TPU v7x, 128 devices: a whole 4x4x4 slice. The times are simulated.
128 devices in a mesh: face: 4 (over y), tile: 32 (over z, x, core).
Axes of the slice: x: 4, y: 4, z: 4, core: 2. Of those that a mesh axis runs over, the one named last changes fastest.
Arguments:
- state: bfloat16 [4, 32, 8, 256, 512], P('face', 'tile'), as said below
- obs_feat: bfloat16 [393216, 128], P(('face', 'tile')), may hold values from -6 to 6
- obs_dest: int32 [393216, 1], P(('face', 'tile')), may hold values from 0 to 127; in each aligned block of 3072 rows (0 to 3071, 3072 to 6143, ...) at most 96 rows name the same one
- obs_cell: int32 [393216], P(('face', 'tile')), may hold values from 0 to 2047
- obs_weight: bfloat16 [128, 512], replicated, may hold values from -0.5 to 0.5
- obs_bias: float32 [512], replicated, may hold values from -3 to 3
- obs_gain: float32 [512], replicated, may hold values from 0.5 to 2
- norm_gain: float32 [512], replicated, may hold values from 0.1 to 1.9
- conv_weight: bfloat16 [9, 512, 512], replicated, may hold values from -0.25 to 0.25
- mlp_gain: float32 [512], replicated, may hold values from 0.1 to 1.9
- mlp_in: bfloat16 [512, 2048], replicated, may hold values from -0.25 to 0.25
- mlp_out: bfloat16 [2048, 512], replicated, may hold values from -0.125 to 0.125
Outputs:
- encoded: bfloat16 [4, 32, 8, 256, 512], P('face', 'tile')
Inputs may be any that keep to these rules, and one draw needn't show every extreme that they name: `obs_dest`: among the rows of one device no strip is named by more than 96 rows, a bound that some block reaches of them. `state`: cell scales differ from cell to cell and channel to channel.
All inputs are finite; a program needn't handle non-finite values.
Results may differ from a plain program's by a relative error of at most 0.0085.
Values may be sent and summed in bfloat16 or wider, within the bound.
A program may use at most 128 MiB of HBM per device.

v0:
```python
import jax
import jax.numpy as jnp
from jax import lax
from jax.sharding import PartitionSpec as P


def from_behind(shard, axis, by):
    length = lax.axis_size(axis)
    return lax.ppermute(shard, axis, [(i, (i + by) % length) for i in range(length)])


def with_halo(block, sides, width):
    for axis, dim in sides:
        count = lax.axis_size(axis)
        forward = [(i, i + 1) for i in range(count - 1)]
        backward = [(target, source) for source, target in forward]
        low = lax.ppermute(
            lax.slice_in_dim(block, block.shape[dim] - width, None, axis=dim), axis, forward
        )
        high = lax.ppermute(lax.slice_in_dim(block, 0, width, axis=dim), axis, backward)
        block = jnp.concatenate([low, block, high], axis=dim)
    return block


def rms_norm(values, gain):
    scale = lax.rsqrt(jnp.mean(values * values, axis=-1, keepdims=True) + 1e-05)
    return values * scale * gain


def shards(
    state,
    obs_feat,
    obs_dest,
    obs_cell,
    obs_weight,
    obs_bias,
    obs_gain,
    norm_gain,
    conv_weight,
    mlp_gain,
    mlp_in,
    mlp_out,
):
    face_count = lax.axis_size("face")
    tile_count = lax.axis_size("tile")
    dev_count = face_count * tile_count
    held_rows = obs_feat.shape[0]
    capacity = 4 * held_rows // dev_count
    block_rows = state.shape[2]
    side = state.shape[3]
    width = state.shape[4]
    cell_count = block_rows * side
    target = obs_dest[:, 0]
    one_hot = (target[:, None] == jnp.arange(dev_count, dtype=jnp.int32)[None, :]).astype(jnp.int32)
    rank_in = jnp.sum(one_hot * jnp.cumsum(one_hot, axis=0), axis=1) - 1
    slot_at = target * capacity + rank_in
    send_rows = (
        jnp.zeros((dev_count * capacity, obs_feat.shape[1]), obs_feat.dtype)
        .at[slot_at]
        .set(obs_feat)
    )
    send_cells = jnp.full((dev_count * capacity,), -1, jnp.int32).at[slot_at].set(obs_cell)
    feats = lax.all_to_all(
        send_rows.reshape(dev_count, capacity, -1),
        ("face", "tile"),
        split_axis=0,
        concat_axis=0,
        tiled=True,
    )
    flat = feats.reshape(-1, feats.shape[-1])
    embed = jax.nn.gelu(jnp.dot(flat, obs_weight, preferred_element_type=jnp.float32) + obs_bias)
    arrived = embed.astype(jnp.bfloat16).reshape(feats.shape[:-1] + (width,))
    spots = lax.all_to_all(
        send_cells.reshape(dev_count, capacity),
        ("face", "tile"),
        split_axis=0,
        concat_axis=0,
        tiled=True,
    )
    arrived = arrived.reshape(-1, width)
    spots = spots.reshape(-1)
    valid = spots >= 0
    seg_index = jnp.where(valid, spots, cell_count)
    total = jax.ops.segment_sum(
        arrived.astype(jnp.float32), seg_index, num_segments=cell_count + 1
    )[:cell_count]
    counted = jax.ops.segment_sum(
        valid.astype(jnp.float32), seg_index, num_segments=cell_count + 1
    )[:cell_count]
    mean_obs = total / jnp.maximum(counted, 1.0)[:, None]
    grid = (
        state[0, 0].astype(jnp.float32) + obs_gain * mean_obs.reshape(block_rows, side, width)
    ).astype(jnp.bfloat16)
    normed = rms_norm(grid.astype(jnp.float32), norm_gain).astype(jnp.bfloat16)
    place = lax.axis_index("tile")
    east_piece = normed[:, side - 1, :]
    top_piece = jnp.where(place == 0, normed[0], jnp.zeros((side, width), jnp.bfloat16))
    east_line, top_all = (
        lax.all_gather(east_piece, "tile", axis=0, tiled=True),
        lax.all_gather(top_piece, "tile", axis=0, tiled=True),
    )
    top_line = top_all.reshape(tile_count, side, width)[0]
    from_prev = from_behind(east_line, "face", 1)
    from_next = from_behind(top_line, "face", -1)
    reversed_next = jnp.pad(from_next[::-1], ((1, 1), (0, 0)))
    seam_east = lax.dynamic_slice_in_dim(reversed_next, place * block_rows, block_rows + 2, 0)
    north_line = jnp.pad(from_prev[::-1], ((1, 1), (0, 0)))
    sides = with_halo(normed, (("tile", 0),), 1)
    zero_col = jnp.zeros((block_rows + 2, 1, width), jnp.bfloat16)
    widened = jnp.concatenate([zero_col, sides, seam_east[:, None]], axis=1)
    top_row = jnp.where(place == 0, north_line, widened[0])
    padded = jnp.concatenate([top_row[None], widened[1:]], axis=0)
    conv = jnp.zeros((cell_count, width), jnp.float32)
    for tap_row in range(3):
        for tap_col in range(3):
            window = padded[tap_row : tap_row + block_rows, tap_col : tap_col + side].reshape(
                -1, width
            )
            conv = conv + jnp.dot(
                window, conv_weight[3 * tap_row + tap_col], preferred_element_type=jnp.float32
            )
    mid = grid.astype(jnp.float32) + conv.reshape(block_rows, side, width)
    normed_two = rms_norm(mid, mlp_gain).astype(jnp.bfloat16)
    hidden = jax.nn.gelu(
        jnp.dot(normed_two.reshape(-1, width), mlp_in, preferred_element_type=jnp.float32)
    ).astype(jnp.bfloat16)
    result = mid + jnp.dot(hidden, mlp_out, preferred_element_type=jnp.float32).reshape(mid.shape)
    return result.astype(jnp.bfloat16)[None, None]


def solution(mesh):
    placed = (
        P("face", "tile", None, None, None),
        P(("face", "tile"), None),
        P(("face", "tile"), None),
        P(("face", "tile")),
        P(),
        P(),
        P(),
        P(),
        P(),
        P(),
        P(),
        P(),
    )
    return jax.shard_map(
        shards,
        mesh=mesh,
        in_specs=placed,
        out_specs=P("face", "tile", None, None, None),
        check_vma=False,
    )
```

profile of v0, /device:TPU:1, one launch (start us, length us, event | category | flops | bytes accessed | tf_op | source)
XLA Modules:
  0.0 397.8 jit_solution(9368010816271836673)
XLA Ops:
  9.2 1.5 broadcast_add_fusion
  11.0 1.9 fusion.45
  12.9 12.0 %scatter_custom_fusion = s32[12288]{0:T(1024)S(1)} fusion(s32[3072]{0:T(1024)S(1)} %bitcast.116, s32[3072]{0:T(1024)} %param.15, s32[]{:T(128)} %constant.17.clone.1), kind=kCustom, calls=%fused_computation.112 | custom fusion | bytes 49664 | tf_op jit(solution)/shard_map/scatter | solution.py:62
  25.6 11.5 %all-to-all-start = ((s32[128,1,96]{2,1,0:T(1,128)}), s32[128,1,96]{2,1,0:T(1,128)S(1)}, u32[]{:S(2)}, u32[]{:S(2)}) async-start(s32[128,1,96]{2,1,0:T(1,128)} %bitcast.7), calls=%async_computation | async-start | bytes 131072 | tf_op jit(solution)/shard_map/all_to_all | solution.py:73
  37.1 10.8 %scatter_custom_fusion.1 = bf16[12288,128]{1,0:T(8,128)(2,1)} fusion(s32[3072]{0:T(1024)S(1)} %bitcast.117, bf16[3072,128]{1,0:T(8,128)(2,1)} %param.13, bf16[]{:T(256)} %constant.22.clone.1), kind=kCustom, calls=%fused_computation.69 | custom fusion | bytes 3146240 | tf_op jit(solution)/shard_map/scatter | solution.py:60
  48.0 10.2 %all-to-all-start.1 = ((bf16[128,96,128]{2,1,0:T(8,128)(2,1)}), bf16[128,96,128]{2,1,0:T(8,128)(2,1)}, u32[]{:S(2)}, u32[]{:S(2)}) async-start(bf16[128,96,128]{2,1,0:T(8,128)(2,1)} %bitcast.98), calls=%async_computation.1 | async-start | bytes 6291456 | tf_op jit(solution)/shard_map/all_to_all | solution.py:63
  60.0 82.7 %scatter_custom_fusion.3 = f32[2049]{0:T(1024)S(1)} fusion(s32[12288]{0:T(1024)S(1)} %bitcast.113, f32[12288]{0:T(1024)S(1)} %reshape.205, f32[]{:T(128)} %constant.16.clone.1), kind=kCustom, calls=%fused_computation.119 | custom fusion | flops 12288 | bytes 8200 | tf_op jit(solution)/shard_map/scatter-add | solution.py:87
  142.8 13.3 %fusion.7 = bf16[12288,512]{1,0:T(8,128)(2,1)} fusion(bf16[12288,128]{1,0:T(8,128)(2,1)} %bitcast.10, bf16[128,512]{1,0:T(8,128)(2,1)S(1)} %copy-done.9, f32[512]{0:T(512)S(1)} %copy-done.10), kind=kOutput, calls=%fused_computation.12 | convolution fusion | flops 1673527296 | bytes 15861760 | tf_op jit(solution)/shard_map/dot_general | solution.py:71
  156.1 86.3 %scatter_custom_fusion.2 = f32[2049,512]{1,0:T(8,128)} fusion(s32[12288]{0:T(1024)S(1)} %bitcast.114, bf16[12288,512]{1,0:T(8,128)(2,1)} %fusion.7, f32[]{:T(128)} %constant.16.clone.1), kind=kCustom, calls=%fused_computation.14 | custom fusion | flops 12582912 | bytes 16779268 | tf_op jit(solution)/shard_map/scatter-add | solution.py:84
  242.4 4.4 %fusion.28 = (bf16[2048,512]{1,0:T(8,128)(2,1)}, f32[2048,512]{1,0:T(8,128)S(1)}) fusion(f32[512]{0:T(512)S(1)} %copy-done.7, bf16[1,1,8,256,512]{4,3,2,1,0:T(8,128)(2,1)} %param.12, f32[2048]{0:T(1024)S(1)} %slice_maximum_fusion, f32[2049,512]{1,0:T(8,128)} %scatter_custom_fusion.2), kind=kLoop, calls=%fused_computation.40 | loop fusion | flops 5242880 | bytes 12593152 | tf_op jit(solution)/shard_map/convert_element_type | solution.py:93
  249.4 1.3 copy-done.1
  252.4 3.3 collective-permute-start.2
  255.8 2.2 collective-permute-start.1
  258.0 24.7 %all-gather = bf16[256,1,512]{2,0,1:T(8,128)(2,1)S(1)} all-gather(bf16[8,1,512]{2,0,1:T(8,128)(2,1)S(1)} %copy.26), channel_id=2, replica_groups=mesh['face'=4,'tile'=32] {'tile'}, dimensions={0}, use_global_device_ids=true | all-gather | bytes 270336 | tf_op jit(solution)/shard_map/all_gather | solution.py:99
  283.9 23.2 %all-gather.4.cloned.1.call-done = bf16[1,8192,512]{2,1,0:T(8,128)(2,1)} async-done(((bf16[1,256,512]{2,1,0:T(8,128)(2,1)}), bf16[1,8192,512]{2,1,0:T(8,128)(2,1)}) %all-gather.4.cloned.1.call-update) | async-done | bytes 8388624 | tf_op jit(solution)/shard_map/all_gather | solution.py:100
  307.1 1.7 slice_bitcast_fusion.1
  308.8 2.6 collective-permute-start.3
  311.4 4.9 %fusion.37 = f32[2048,512]{1,0:T(8,128)} fusion(bf16[2048,512]{1,0:T(8,128)(2,1)} %get-tuple-element.5, f32[512]{0:T(512)S(1)} %copy-done.8, f32[2048]{0:T(1024)S(1)} %bitcast.118, bf16[9,512,512]{2,1,0:T(8,128)(2,1)} %param.20), kind=kOutput, calls=%fused_computation.60 | convolution fusion | flops 1077936128 | bytes 6825984 | tf_op jit(solution)/shard_map/dot_general | solution.py:119
  316.3 3.2 rev.6
  319.5 3.0 pad_maximum_fusion.2
  322.5 3.2 rev.7
  325.8 2.7 pad_maximum_fusion
  333.4 3.2 fusion.65
  336.7 3.1 fusion.33
  339.8 1.6 fusion.90
  341.4 3.2 fusion.51
  344.6 3.2 fusion.54
  347.8 3.2 fusion.56
  351.0 3.2 fusion.59
  354.2 14.7 %multiply_reduce_fusion = (f32[2048]{0:T(1024)S(1)}, f32[2048,512]{1,0:T(8,128)}) fusion(bf16[2048,512]{1,0:T(8,128)(2,1)} %get-tuple-element.5, f32[2048,512]{1,0:T(8,128)} %fusion.51, bf16[2048,512]{1,0:T(8,128)(2,1)} %bitcast.106, bf16[9,512,512]{2,1,0:T(8,128)(2,1)} %param.20, f32[2048,512]{1,0:T(8,128)} %fusion.54, f32[2048,512]{1,0:T(8,128)} %fusion.56, ...), kind=kOutput, calls=%fused_computation.45 | convolution fusion | flops 1086322688 | bytes 42475520 | tf_op jit(solution)/shard_map/dot_general | solution.py:119
  368.9 13.5 %fusion.18 = f32[2048,512]{1,0:T(8,128)} fusion(bf16[2048,512]{1,0:T(8,128)(2,1)S(1)} %copy-done, bf16[512,2048]{1,0:T(8,128)(2,1)} %param.22, f32[2048,512]{1,0:T(8,128)} %get-tuple-element.24, bf16[2048,512]{1,0:T(8,128)(2,1)} %get-tuple-element.5, f32[512]{0:T(512)S(1)} %copy-done.11, f32[2048]{0:T(1024)S(1)} %add_rsqrt_fusion), kind=kOutput, calls=%fused_computation.24 | convolution fusion | flops 8632926208 | bytes 14690304 | tf_op jit(solution)/shard_map/dot_general | solution.py:127
  382.4 8.4 %add_convert_fusion = bf16[1,1,8,256,512]{4,3,2,1,0:T(8,128)(2,1)} fusion(f32[1,1,8,256,512]{4,3,2,1,0:T(8,128)} %bitcast.107, f32[1,1,8,256,512]{4,3,2,1,0:T(8,128)} %bitcast.97, f32[1,1,8,256,512]{4,3,2,1,0:T(8,128)} %bitcast.96, f32[512]{0:T(512)S(1)} %copy-done.7, bf16[1,1,8,256,512]{4,3,2,1,0:T(8,128)(2,1)} %param.12), kind=kLoop, calls=%fused_computation.43 | loop fusion | flops 8388608 | bytes 16779264 | tf_op jit(solution)/shard_map/convert_element_type | solution.py:128
  (69 shorter events, 15.8 us)
Async XLA Ops:
  6.5 362.3 %copy-start = (bf16[2048,512]{1,0:T(8,128)(2,1)S(1)}, bf16[2048,512]{1,0:T(8,128)(2,1)}, u32[]{:S(2)}) copy-start(bf16[2048,512]{1,0:T(8,128)(2,1)} %param.23) | copy-start | bytes 6291460
  6.5 4.5 %copy-start.6 = (s32[3072,1]{0,1:T(1,128)S(1)}, s32[3072,1]{0,1:T(1,128)}, u32[]{:S(2)}) copy-start(s32[3072,1]{0,1:T(1,128)} %param.14) | copy-start | bytes 36868
  8.0 1.1 copy-start.5
  25.6 22.3 %all-to-all-start = ((s32[128,1,96]{2,1,0:T(1,128)}), s32[128,1,96]{2,1,0:T(1,128)S(1)}, u32[]{:S(2)}, u32[]{:S(2)}) async-start(s32[128,1,96]{2,1,0:T(1,128)} %bitcast.7), calls=%async_computation | async-start | bytes 131072 | tf_op jit(solution)/shard_map/all_to_all | solution.py:73
  48.0 94.8 %copy-start.9 = (bf16[128,512]{1,0:T(8,128)(2,1)S(1)}, bf16[128,512]{1,0:T(8,128)(2,1)}, u32[]{:S(2)}) copy-start(bf16[128,512]{1,0:T(8,128)(2,1)} %param.16) | copy-start | bytes 393220
  48.0 94.8 %copy-start.10 = (f32[512]{0:T(512)S(1)}, f32[512]{0:T(512)}, u32[]{:S(2)}) copy-start(f32[512]{0:T(512)} %param.17) | copy-start | bytes 6148
  48.0 94.8 %all-to-all-start.1 = ((bf16[128,96,128]{2,1,0:T(8,128)(2,1)}), bf16[128,96,128]{2,1,0:T(8,128)(2,1)}, u32[]{:S(2)}, u32[]{:S(2)}) async-start(bf16[128,96,128]{2,1,0:T(8,128)(2,1)} %bitcast.98), calls=%async_computation.1 | async-start | bytes 6291456 | tf_op jit(solution)/shard_map/all_to_all | solution.py:63
  58.1 249.0 %all-gather.4.cloned.1.call-start = ((), (), s32[]{:S(2)}) async-start(), calls=%async_computation.2 | async-start | bytes 8650752 | tf_op jit(solution)/shard_map/all_gather | solution.py:100
  156.1 86.3 %copy-start.7 = (f32[512]{0:T(512)S(1)}, f32[512]{0:T(512)}, u32[]{:S(2)}) copy-start(f32[512]{0:T(512)} %param.18) | copy-start | bytes 6148
  242.4 4.4 %copy-start.4 = (bf16[1,1,8,256,512]{4,3,2,1,0:T(8,128)(2,1)S(1)}, bf16[1,1,8,256,512]{4,3,2,1,0:T(8,128)(2,1)}, u32[]{:S(2)}) copy-start(bf16[1,1,8,256,512]{4,3,2,1,0:T(8,128)(2,1)} %param.12) | copy-start | bytes 6291460
  246.8 1.9 copy-start.3
  246.8 1.9 copy-start.8
  249.3 1.3 copy-start.1
  252.4 67.1 %collective-permute-start.2 = (bf16[1,256,512]{2,1,0:T(8,128)(2,1)S(1)}, bf16[1,256,512]{2,1,0:T(8,128)(2,1)S(1)}, u32[]{:S(2)}, u32[]{:S(2)}) collective-permute-start(bf16[1,256,512]{2,1,0:T(8,128)(2,1)S(1)} %get-tuple-element.20), channel_id=1, source_target_pairs={{1,0},{2,1},{3,2},{4,3},{5,4},{6,5},{7,6},{8,7},{9,8},{10,9},{11,1... | collective-permute-start | bytes 786440 | tf_op jit(solution)/shard_map/ppermute | solution.py:20
  255.8 70.0 %collective-permute-start.1 = (bf16[1,256,512]{2,1,0:T(8,128)(2,1)}, bf16[1,256,512]{2,1,0:T(8,128)(2,1)S(1)}, u32[]{:S(2)}, u32[]{:S(2)}) collective-permute-start(bf16[1,256,512]{2,1,0:T(8,128)(2,1)} %get-tuple-element.18), channel_id=1, source_target_pairs={{0,1},{1,2},{2,3},{3,4},{4,5},{5,6},{6,7},{7,8},{8,9},{9,10},{10,1... | collective-permute-start | bytes 786440 | tf_op jit(solution)/shard_map/ppermute | solution.py:17
  282.8 33.5 %collective-permute-start = (bf16[256,512]{1,0:T(8,128)(2,1)S(1)}, bf16[256,512]{1,0:T(8,128)(2,1)}, u32[]{:S(2)}, u32[]{:S(2)}) collective-permute-start(bf16[256,512]{1,0:T(8,128)(2,1)S(1)} %bitcast.110), channel_id=1, source_target_pairs={{0,32},{32,64},{64,96},{96,0},{1,33},{33,65},{65,97},{97,1},{2,34}... | collective-permute-start | bytes 786440 | tf_op jit(solution)/shard_map/ppermute | solution.py:9
  308.8 13.8 %collective-permute-start.3 = (bf16[256,512]{1,0:T(8,128)(2,1)}, bf16[256,512]{1,0:T(8,128)(2,1)}, u32[]{:S(2)}, u32[]{:S(2)}) collective-permute-start(bf16[256,512]{1,0:T(8,128)(2,1)} %slice_bitcast_fusion.1), channel_id=1, source_target_pairs={{0,96},{32,0},{64,32},{96,64},{1,97},{33,1},{65,33},{97,65},{2,98}... | collective-permute-start | bytes 786440 | tf_op jit(solution)/shard_map/ppermute | solution.py:9
  328.5 2.2 slice-start
  328.8 2.1 slice-start.1
  333.4 3.3 copy-start.2
  354.2 14.7 %copy-start.11 = (f32[512]{0:T(512)S(1)}, f32[512]{0:T(512)}, u32[]{:S(2)}) copy-start(f32[512]{0:T(512)} %param.21) | copy-start | bytes 6148
Sparse Core Ops, SparseCore 0:
  251.7 55.3 all-gather.3
where the time goes:
time: 406 us; the launch traced here: 398 us
  other arithmetic  199 us (49%)
  matrix products  64.9 us (16%)
  local copies, waits for them, and re-layouts  40.7 us (10%)
  starting transfers between devices  31 us (8%)
  blocking collectives  24.7 us (6%)
  waiting for transfers between devices  23.2 us (6%)
  between operations  14 us (3%)
    scatter-add x1, other arithmetic, shards(): jax.ops.segment_sum(arrived.astype(jnp.float32), seg_index, num_segments=...  86.3 us
    scatter-add x1, other arithmetic, shards(): jax.ops.segment_sum(valid.astype(jnp.float32), seg_index, num_segments=ce...  82.7 us
    dot_general x9, matrix products, shards(): jnp.dot(window, conv_weight[3 * tap_row + tap_col], preferred_element_typ...  38.1 us
    all_gather x1, blocking collectives, shards(): lax.all_gather(east_piece, 'tile', axis=0, tiled=True)  24.7 us
    all_gather x1, waiting for transfers between devices, shards(): lax.all_gather(top_piece, 'tile', axis=0, tiled=True)  23.2 us
    dot_general x1, matrix products, shards(): jnp.dot(hidden, mlp_out, preferred_element_type=jnp.float32)  13.5 us
    dot_general x1, matrix products, shards(): jnp.dot(flat, obs_weight, preferred_element_type=jnp.float32) + obs_bias  13.3 us
    scatter x1, local copies, waits for them, and re-layouts, shards(): jnp.full((dev_count * capacity,), -1, jnp.int32).at[slot_at].set(obs_cell)  12 us
  transfers between devices with their start and end apart: 7, of which 1 were waited for; matrix products, arithmetic and copies ran while one was open for 28% of the time, Pallas kernels for 0%

commit v1 on v0

v1 whole, which is shorter than its diff:
```python
import math

import jax
import jax.numpy as jnp
from jax import lax
from jax.experimental import pallas as pl
from jax.experimental.pallas import tpu as pltpu
from jax.sharding import PartitionSpec as P

BF16 = jnp.bfloat16
F32 = jnp.float32
I32 = jnp.int32
MESH = pl.DeviceIdType.MESH
EPS = 1e-05
MIB = 2**20
UNIT = 16
BLOCK = 256


def gelu(x):
    inner = x * (math.sqrt(2.0 / math.pi) + (0.044715 * math.sqrt(2.0 / math.pi)) * (x * x))
    half = 0.5 * x
    return half + half * jnp.tanh(inner)


def ones_where(mask):
    return jnp.where(mask, 1.0, 0.0)


def dot(a, b):
    return jnp.dot(a, b, preferred_element_type=F32)


def dot_lanes(a, b):
    return lax.dot_general(a, b, (((1,), (1,)), ((), ())), preferred_element_type=F32)


def rank_kernel(dest, cell, rank, starts, cells):
    devices = starts.shape[1]
    rows = dest.shape[1]
    hot = lax.broadcasted_iota(I32, (devices, rows), 0) == dest[...]
    hot_f = ones_where(hot)
    hot_b = hot_f.astype(BF16)
    before = ones_where(
        lax.broadcasted_iota(I32, (BLOCK, BLOCK), 0) < lax.broadcasted_iota(I32, (BLOCK, BLOCK), 1)
    ).astype(BF16)
    ahead = jnp.zeros((devices, 1), F32)
    pieces = []
    for block in range(rows // BLOCK):
        at = slice(block * BLOCK, (block + 1) * BLOCK)
        pieces.append(dot(hot_b[:, at], before) + ahead)
        ahead = ahead + jnp.sum(hot_f[:, at], axis=1, keepdims=True)
    earlier = jnp.concatenate(pieces, axis=1)
    row_id = lax.broadcasted_iota(I32, (devices, devices), 0)
    col_id = lax.broadcasted_iota(I32, (devices, devices), 1)
    start = dot(
        ones_where(col_id < row_id).astype(BF16),
        jnp.broadcast_to(ahead, (devices, devices)).astype(BF16),
    )
    starts[...] = jnp.sum(jnp.where(row_id == col_id, start, 0.0), axis=0, keepdims=True).astype(I32)
    rank_in = jnp.sum(hot_f * earlier, axis=0, keepdims=True).astype(I32)
    rank[...] = jnp.sum(hot_f * (earlier + start[:, :1]), axis=0, keepdims=True).astype(I32)
    spot = cell[...] + 1
    high = hot_f * (spot // 128).astype(F32)
    low = hot_f * (spot % 128).astype(F32)
    in_slot = ones_where(lax.broadcasted_iota(I32, (128, rows), 0) == rank_in).astype(BF16)
    split = dot_lanes(jnp.concatenate([high, low], axis=0).astype(BF16), in_slot)
    cells[...] = (split[:devices] * 128.0 + split[devices:]).astype(I32)


def cut_kernel(starts, rank, feat, send, ordered):
    devices = send.shape[0]
    rows = feat.shape[0]
    capacity = send.shape[1] * send.shape[2]

    def sort_block(block, _):
        first = pl.multiple_of(block * BLOCK, BLOCK)
        chosen = ones_where(
            lax.broadcasted_iota(I32, (BLOCK, rows), 0) + first == rank[...]
        ).astype(BF16)
        ordered[pl.ds(first, BLOCK), :] = dot(chosen, feat[...])
        return 0

    lax.fori_loop(0, rows // BLOCK, sort_block, 0)
    ordered[rows:, :] = jnp.zeros((ordered.shape[0] - rows, feat.shape[1]), F32)

    def cut(target, _):
        values = ordered[pl.ds(starts[0, target], capacity), :]
        send[target] = values.astype(BF16).reshape(send.shape[1:])
        return 0

    lax.fori_loop(0, devices, cut, 0, unroll=4)


def pack(dest, cell, feat, devices, capacity):
    rows, width = feat.shape
    vmem = pl.BlockSpec(memory_space=pltpu.VMEM)
    rank, starts, cells = pl.pallas_call(
        rank_kernel,
        out_shape=(
            jax.ShapeDtypeStruct((1, rows), I32),
            jax.ShapeDtypeStruct((1, devices), I32),
            jax.ShapeDtypeStruct((devices, 128), I32),
        ),
        in_specs=[vmem] * 2,
        out_specs=[vmem] * 3,
        compiler_params=pltpu.CompilerParams(vmem_limit_bytes=40 * MIB),
        name="rank",
    )(dest, cell)
    send = pl.pallas_call(
        cut_kernel,
        out_shape=jax.ShapeDtypeStruct((devices, capacity // UNIT, UNIT, width), BF16),
        in_specs=[pl.BlockSpec(memory_space=pltpu.SMEM), vmem, vmem],
        out_specs=vmem,
        scratch_shapes=[pltpu.VMEM((rows + 2 * capacity, width), F32)],
        compiler_params=pltpu.CompilerParams(vmem_limit_bytes=40 * MIB),
        name="cut",
    )(starts, rank, feat)
    return send, cells


def spread_cells(cells, part):
    sources = cells.shape[0]
    lane = lax.broadcasted_iota(I32, (128, 128), 1)
    pick = ones_where(
        lax.broadcasted_iota(I32, (128, 128), 0) == lane % UNIT + part * UNIT
    ).astype(BF16)
    high = dot((cells // 128).astype(F32).astype(BF16), pick)
    low = dot((cells % 128).astype(F32).astype(BF16), pick)
    value = high * 128.0 + low
    keep = lax.broadcasted_iota(I32, (sources, 128), 1) // UNIT == (
        lax.broadcasted_iota(I32, (sources, 128), 0) % 8
    )
    value = jnp.where(keep, value, 0.0).reshape(sources // 8, 8, 128)
    return jnp.sum(value, axis=1).astype(I32) - 1


def add_part(feats, spots, weight, bias, embed, total, count):
    slots = feats.shape[0]
    for block in range(slots // 512):
        at = slice(block * 512, (block + 1) * 512)
        embed[at, :] = gelu(dot(feats[at], weight[...]) + bias[...]).astype(BF16)

    def cell_block(block, _):
        first = pl.multiple_of(block * BLOCK, BLOCK)
        ids = lax.broadcasted_iota(I32, (BLOCK, 128), 0) + first
        hits = [ones_where(ids == spots[group : group + 1, :]) for group in range(slots // 128)]
        seen = hits[0]
        for hit in hits[1:]:
            seen = seen + hit
        match = jnp.concatenate([hit.astype(BF16) for hit in hits], axis=1)
        total[pl.ds(first, BLOCK), :] += dot(match, embed[...])
        count[pl.ds(first, BLOCK), :] += seen
        return 0

    lax.fori_loop(0, total.shape[0] // BLOCK, cell_block, 0)


def finish_grid(state, obs_gain, norm_gain, total, count, grid, normed):
    def block_of(block, _):
        at = pl.ds(pl.multiple_of(block * BLOCK, BLOCK), BLOCK)
        number = jnp.maximum(jnp.sum(count[at, :], axis=1, keepdims=True), 1.0)
        value = state[at, :].astype(F32) + obs_gain[...] * (total[at, :] * (1.0 / number))
        rounded = value.astype(BF16)
        grid[at, :] = rounded
        value = rounded.astype(F32)
        scale = lax.rsqrt(jnp.mean(value * value, axis=1, keepdims=True) + EPS)
        normed[at, :] = (value * scale * norm_gain[...]).astype(BF16)
        return 0

    lax.fori_loop(0, total.shape[0] // BLOCK, block_of, 0)


def assimilate_kernel(
    arrived, cells, state, weight, bias, obs_gain, norm_gain, grid, normed, embed, total, count, spots
):
    parts = arrived.shape[1]
    sources = arrived.shape[0]
    total[...] = jnp.zeros_like(total)
    count[...] = jnp.zeros_like(count)
    for part in range(parts):
        spots[part] = spread_cells(cells[...], part)

    def one(part, _):
        feats = arrived[:, part].reshape(sources * UNIT, arrived.shape[3])
        add_part(feats, spots.at[part], weight, bias, embed, total, count)
        return 0

    lax.fori_loop(0, parts, one, 0)
    finish_grid(state, obs_gain, norm_gain, total, count, grid, normed)


def assimilate(arrived, cells, state, weight, bias, obs_gain, norm_gain):
    cell_count, width = state.shape
    sources, parts = arrived.shape[:2]
    return pl.pallas_call(
        assimilate_kernel,
        out_shape=(jax.ShapeDtypeStruct(state.shape, BF16),) * 2,
        in_specs=[pl.BlockSpec(memory_space=pltpu.VMEM)] * 7,
        out_specs=[pl.BlockSpec(memory_space=pltpu.VMEM)] * 2,
        scratch_shapes=[
            pltpu.VMEM((sources * UNIT, width), BF16),
            pltpu.VMEM((cell_count, width), F32),
            pltpu.VMEM((cell_count, 128), F32),
            pltpu.VMEM((parts, sources // 8, 128), I32),
        ],
        compiler_params=pltpu.CompilerParams(vmem_limit_bytes=50 * MIB),
        name="assimilate",
    )(arrived, cells, state, weight, bias, obs_gain, norm_gain)


def halo_kernel(
    normed, north, south, seam, edges, east_block, seam_out, above, below, from_east, seam_in,
    up_sems, down_sems, east_send, east_recv, seam_send, seam_recv,
):
    faces, tiles = lax.axis_size("face"), lax.axis_size("tile")
    face, tile = lax.axis_index("face"), lax.axis_index("tile")
    cell_count, width = normed.shape
    side = above.shape[0]
    rows = cell_count // side
    following, preceding = lax.rem(face + 1, faces), lax.rem(face + faces - 1, faces)
    is_first, is_last = tile == 0, tile == tiles - 1
    barrier = pltpu.get_barrier_semaphore()

    def greet(who):
        pl.semaphore_signal(barrier, inc=1, device_id=who, device_id_type=MESH)

    greet((following, 0))

    @pl.when(jnp.logical_not(is_first))
    def _():
        greet((face, tile - 1))

    @pl.when(jnp.logical_not(is_last))
    def _():
        greet((face, tile + 1))

    @pl.when(is_first)
    def _():
        def one(other, _):
            greet((preceding, other))
            return 0

        lax.fori_loop(0, tiles, one, 0)

    edges[0] = normed[0:side, :]
    edges[1] = normed[cell_count - side : cell_count, :]
    for row in range(rows):
        last = normed[(rows - row) * side - 16 : (rows - row) * side, :].astype(F32)
        east_block[row : row + 1, :] = last[15:16, :]

    @pl.when(is_first)
    def _():
        slot = lax.broadcasted_iota(I32, (tiles * UNIT, side), 0)
        want = side - 1 - (slot // UNIT * rows - 1 + slot % UNIT)
        chosen = ones_where(lax.broadcasted_iota(I32, (tiles * UNIT, side), 1) == want)
        seam_out[...] = dot(chosen.astype(BF16), normed[0:side, :]).astype(BF16).reshape(
            tiles, UNIT, width
        )

    partners = 1 + jnp.where(is_first, tiles, 1) + jnp.where(is_last, 0, 1)
    pl.semaphore_wait(barrier, partners)

    up = pltpu.make_async_remote_copy(
        src_ref=edges.at[0], dst_ref=below,
        send_sem=up_sems.at[0], recv_sem=up_sems.at[1],
        device_id=(face, jnp.maximum(tile - 1, 0)), device_id_type=MESH,
    )
    down = pltpu.make_async_remote_copy(
        src_ref=edges.at[1], dst_ref=above,
        send_sem=down_sems.at[0], recv_sem=down_sems.at[1],
        device_id=(face, jnp.minimum(tile + 1, tiles - 1)), device_id_type=MESH,
    )
    east = pltpu.make_async_remote_copy(
        src_ref=east_block, dst_ref=from_east.at[tiles - 1 - tile],
        send_sem=east_send, recv_sem=east_recv.at[tile],
        device_id=(following, 0), device_id_type=MESH,
    )

    def seam_copy(other):
        return pltpu.make_async_remote_copy(
            src_ref=seam_out.at[other], dst_ref=seam_in,
            send_sem=seam_send.at[other], recv_sem=seam_recv,
            device_id=(preceding, other), device_id_type=MESH,
        )

    @pl.when(is_first)
    def _():
        def one(other, _):
            seam_copy(other).start()
            return 0

        lax.fori_loop(0, tiles, one, 0)

    east.start()

    @pl.when(jnp.logical_not(is_first))
    def _():
        up.start()

    @pl.when(jnp.logical_not(is_last))
    def _():
        down.start()

    @pl.when(jnp.logical_not(is_last))
    def _():
        up.wait_recv()
        south[...] = below[...]
        down.wait_send()

    @pl.when(is_last)
    def _():
        south[...] = jnp.zeros_like(south)

    @pl.when(jnp.logical_not(is_first))
    def _():
        down.wait_recv()
        north[...] = above[...]
        up.wait_send()

    east.wait_send()
    pltpu.make_async_remote_copy(
        src_ref=seam_out.at[0], dst_ref=seam_in,
        send_sem=seam_send.at[0], recv_sem=seam_recv,
        device_id=(following, 0), device_id_type=MESH,
    ).wait_recv()
    seam[...] = seam_in[...].astype(F32)

    @pl.when(is_first)
    def _():
        def one(other, _):
            seam_copy(other).wait_send()
            pltpu.make_async_remote_copy(
                src_ref=east_block, dst_ref=from_east.at[tiles - 1 - other],
                send_sem=east_send, recv_sem=east_recv.at[other],
                device_id=(preceding, other), device_id_type=MESH,
            ).wait_recv()
            return 0

        lax.fori_loop(0, tiles, one, 0)
        north[...] = from_east[...].reshape(side, width).astype(BF16)


def exchange_halo(normed, tiles, rows):
    cell_count, width = normed.shape
    side = cell_count // rows
    return pl.pallas_call(
        halo_kernel,
        out_shape=(
            jax.ShapeDtypeStruct((side, width), BF16),
            jax.ShapeDtypeStruct((side, width), BF16),
            jax.ShapeDtypeStruct((UNIT, width), F32),
        ),
        in_specs=[pl.BlockSpec(memory_space=pltpu.VMEM)],
        out_specs=[pl.BlockSpec(memory_space=pltpu.VMEM)] * 3,
        scratch_shapes=[
            pltpu.VMEM((2, side, width), BF16),
            pltpu.VMEM((rows, width), F32),
            pltpu.VMEM((tiles, UNIT, width), BF16),
            pltpu.VMEM((side, width), BF16),
            pltpu.VMEM((side, width), BF16),
            pltpu.VMEM((tiles, rows, width), F32),
            pltpu.VMEM((UNIT, width), BF16),
            pltpu.SemaphoreType.DMA((2,)),
            pltpu.SemaphoreType.DMA((2,)),
            pltpu.SemaphoreType.DMA,
            pltpu.SemaphoreType.DMA((tiles,)),
            pltpu.SemaphoreType.DMA((tiles,)),
            pltpu.SemaphoreType.DMA,
        ],
        compiler_params=pltpu.CompilerParams(
            collective_id=1, has_side_effects=True, vmem_limit_bytes=30 * MIB
        ),
        name="halo",
    )(normed)


def block_kernel(
    normed, north, south, seam, grid, conv_weight, mlp_gain, mlp_in, mlp_out, out, planes, *, per
):
    step = pl.program_id(0)
    steps = pl.num_programs(0)
    side, width = north.shape
    hidden_step = 512

    def put(row, values):
        values = values.astype(F32)
        at = lax.broadcasted_iota(I32, (side, width), 0)
        left = jnp.where(at == 0, 0.0, pltpu.roll(values, 1, 0))
        right = jnp.where(at == side - 1, seam[pl.ds(row, 1), :], pltpu.roll(values, side - 1, 0))
        planes[row, :, 0:width] = left.astype(BF16)
        planes[row, :, width : 2 * width] = values.astype(BF16)
        planes[row, :, 2 * width : 3 * width] = right.astype(BF16)

    def strip_row(row):
        return normed[pl.ds(pl.multiple_of(row * side, side), side), :]

    @pl.when(step == 0)
    def _():
        put(0, north[...])
        put(1, normed[0:side, :])

    for ahead in range(per):
        row = step * per + 2 + ahead
        if ahead < per - 1:
            put(row, strip_row(row - 1))
        else:
            inner = strip_row(jnp.minimum(row - 1, steps * per - 1))
            put(row, jnp.where(step == steps - 1, south[...], inner))

    conv = None
    for tap in range(3):
        window = planes[pl.ds(step * per + tap, per)].reshape(per * side, 3 * width)
        term = dot(window, conv_weight[tap])
        conv = term if conv is None else conv + term
    mid = grid[...].astype(F32) + conv
    scale = lax.rsqrt(jnp.mean(mid * mid, axis=1, keepdims=True) + EPS)
    normed_two = (mid * scale * mlp_gain[...]).astype(BF16)
    result = mid
    for part in range(mlp_in.shape[1] // hidden_step):
        at = slice(part * hidden_step, (part + 1) * hidden_step)
        hidden = gelu(dot(normed_two, mlp_in[:, at])).astype(BF16)
        result = result + dot(hidden, mlp_out[at, :])
    out[...] = result.astype(BF16)


def encode(normed, north, south, seam, grid, conv_weight, mlp_gain, mlp_in, mlp_out, per=2):
    cell_count, width = normed.shape
    side = north.shape[0]
    rows = cell_count // side
    whole = pl.BlockSpec(memory_space=pltpu.VMEM)
    strip = pl.BlockSpec((per * side, width), lambda i: (i, 0))

    def body(*refs):
        block_kernel(*refs, per=per)

    return pl.pallas_call(
        body,
        grid=(rows // per,),
        out_shape=jax.ShapeDtypeStruct(normed.shape, BF16),
        in_specs=[whole, whole, whole, whole, strip, whole, whole, whole, whole],
        out_specs=strip,
        scratch_shapes=[pltpu.VMEM((rows + 2, side, 3 * width), BF16)],
        compiler_params=pltpu.CompilerParams(vmem_limit_bytes=56 * MIB),
        name="encode",
    )(normed, north, south, seam, grid, conv_weight, mlp_gain, mlp_in, mlp_out)


def encode_plain(normed, north, south, seam, grid, conv_weight, mlp_gain, mlp_in, mlp_out):
    cell_count, width = normed.shape
    side = north.shape[0]
    rows = cell_count // side
    sides = jnp.concatenate([north, normed, south]).reshape(rows + 2, side, width)
    zero_col = jnp.zeros((rows + 2, 1, width), BF16)
    seam = seam[: rows + 2, None].astype(BF16)
    padded = jnp.concatenate([zero_col, sides, seam], axis=1)
    conv = jnp.zeros((cell_count, width), F32)
    for tap_row in range(3):
        for tap_col in range(3):
            window = padded[tap_row : tap_row + rows, tap_col : tap_col + side].reshape(-1, width)
            conv = conv + dot(window, conv_weight[3 * tap_row + tap_col])
    mid = grid.astype(F32) + conv
    scale = lax.rsqrt(jnp.mean(mid * mid, axis=-1, keepdims=True) + EPS)
    normed_two = (mid * scale * mlp_gain).astype(BF16)
    hidden = jax.nn.gelu(dot(normed_two, mlp_in)).astype(BF16)
    return (mid + dot(hidden, mlp_out)).astype(BF16)


def shards(
    state,
    obs_feat,
    obs_dest,
    obs_cell,
    obs_weight,
    obs_bias,
    obs_gain,
    norm_gain,
    conv_weight,
    mlp_gain,
    mlp_in,
    mlp_out,
):
    tiles = lax.axis_size("tile")
    devices = lax.axis_size("face") * tiles
    held = obs_feat.shape[0]
    capacity = 4 * held // devices
    rows, side, width = state.shape[2:]
    send, cells = pack(
        obs_dest.reshape(1, held), obs_cell.reshape(1, held), obs_feat, devices, capacity
    )
    arrived = lax.all_to_all(send, ("face", "tile"), split_axis=0, concat_axis=0, tiled=True)
    cells = lax.all_to_all(cells, ("face", "tile"), split_axis=0, concat_axis=0, tiled=True)
    grid, normed = assimilate(
        arrived,
        cells,
        state.reshape(rows * side, width),
        obs_weight,
        obs_bias.reshape(1, width),
        obs_gain.reshape(1, width),
        norm_gain.reshape(1, width),
    )
    north, south, seam = exchange_halo(normed, tiles, rows)
    result = encode_plain(
        normed,
        north,
        south,
        seam,
        grid,
        conv_weight,
        mlp_gain.reshape(1, width),
        mlp_in,
        mlp_out,
    )
    return result.reshape(state.shape)


def solution(mesh):
    placed = (
        P("face", "tile", None, None, None),
        P(("face", "tile"), None),
        P(("face", "tile"), None),
        P(("face", "tile")),
    ) + (P(),) * 8
    return jax.shard_map(
        shards,
        mesh=mesh,
        in_specs=placed,
        out_specs=P("face", "tile", None, None, None),
        check_vma=False,
    )
```

time: 406 us -> 206 us (0.51)
  the two profiles are of different devices: /device:TPU:1 before, /device:TPU:0 now
where the time goes in v1:
time: 206 us; the launch traced here: 205 us
  Pallas kernels  71.8 us (35%)
  matrix products  58.9 us (29%)
  blocking collectives  51.5 us (25%)
  starting transfers between devices  11.1 us (5%)
  local copies, waits for them, and re-layouts  5.98 us (3%)
  other arithmetic  5.82 us (3%)
    dot_general x10, matrix products, dot(): return jnp.dot(a, b, preferred_element_type=F32)  58.9 us
    all_to_all x1, blocking collectives, shards(): lax.all_to_all(send, ('face', 'tile'), split_axis=0, concat_axis=0, tiled...  51.5 us
    pallas_call x1, Pallas kernels, assimilate(): pl.pallas_call(assimilate_kernel, out_shape=(jax.ShapeDtypeStruct(state.s...  50.4 us
    pallas_call x1, Pallas kernels, exchange_halo(): pl.pallas_call(halo_kernel, out_shape=(jax.ShapeDtypeStruct((side, width)...  11.6 us
    all_to_all x1, starting transfers between devices, shards(): lax.all_to_all(cells, ('face', 'tile'), split_axis=0, concat_axis=0, tile...  11.1 us
    pallas_call x1, Pallas kernels, pack(): pl.pallas_call(cut_kernel, out_shape=jax.ShapeDtypeStruct((devices, capac...  7.73 us
    unnamed x24, local copies, waits for them, and re-layouts  5.96 us
  transfers between devices with their start and end apart: 1, of which 0 were waited for; matrix products, arithmetic and copies ran while one was open for 0% of the time, Pallas kernels for 4%

profile of v1, /device:TPU:0, one launch (start us, length us, event | category | flops | bytes accessed | tf_op | source)
XLA Modules:
  0.0 205.2 jit_solution(276625943699303543)
XLA Ops:
  0.0 0.0 copy-start
  0.0 0.9 copy-done.6
  0.9 0.7 copy-done.7
  1.6 2.0 rank.1
  3.6 11.1 %all-to-all-start.1 = ((s32[128,1,128]{2,1,0:T(1,128)}), s32[128,1,128]{2,1,0:T(1,128)S(1)}, u32[]{:S(2)}, u32[]{:S(2)}) async-start(s32[128,1,128]{2,1,0:T(1,128)} %bitcast.3), calls=%async_computation.1 | async-start | bytes 131072 | tf_op jit(solution)/shard_map/all_to_all | solution.py:492
  14.7 0.0 copy-start.4
  14.8 1.1 copy-done.4
  15.9 7.7 %cut.1 = bf16[128,6,16,128]{3,2,1,0:T(8,128)(2,1)S(1)} custom-call(s32[1,128]{1,0:T(1,128)S(1)} %get-tuple-element.13.starts, s32[1,3072]{1,0:T(1,128)S(1)} %get-tuple-element.14.rank, bf16[3072,128]{1,0:T(8,128)(2,1)S(1)} %copy-done.4), custom_call_target="tpu_custom_call" | custom-call | tf_op jit(solution)/shard_map/cut/pallas_call | solution.py:110
  23.6 0.0 copy-start.3
  23.6 1.6 copy-done.3
  25.3 0.0 all-to-all-done.1
  25.3 51.5 %all_to_all.16.arrived = bf16[128,6,16,128]{3,2,1,0:T(8,128)(2,1)} all-to-all(bf16[128,6,16,128]{3,2,1,0:T(8,128)(2,1)} %copy-done.3), channel_id=1, replica_groups=mesh['face'=4,'tile'=32] {'face','tile'}, dimensions={0} | all-to-all | bytes 6291456 | tf_op jit(solution)/shard_map/all_to_all | solution.py:491
  76.8 0.0 copy-done.5
  76.8 0.0 copy-done.8
  76.8 0.0 copy-done.9
  76.8 50.4 %assimilate.1 = (bf16[2048,512]{1,0:T(8,128)(2,1)S(1)}, bf16[2048,512]{1,0:T(8,128)(2,1)}) custom-call(bf16[128,6,16,128]{3,2,1,0:T(8,128)(2,1)} %all_to_all.16.arrived, s32[128,128]{1,0:T(8,128)S(1)} %bitcast.58, bf16[2048,512]{1,0:T(8,128)(2,1)} %bitcast.71, bf16[128,512]{1,0:T(8,128)(2,1)S(1)} %copy-done.5, f32[1,512]{1,0:T(1,128)S(1)} %bitcast.61, ...), custom_call_target="tpu_custom_call" | custom-call | tf_op jit(solution)/shard_map/assimilate/pallas_call | solution.py:196
  127.2 1.6 copy-done.1
  128.8 11.6 %halo.1 = (bf16[256,512]{1,0:T(8,128)(2,1)S(1)}, bf16[256,512]{1,0:T(8,128)(2,1)S(1)}, f32[16,512]{1,0:T(8,128)S(1)}) custom-call(bf16[2048,512]{1,0:T(8,128)(2,1)S(1)} %copy-done.1), custom_call_target="tpu_custom_call" | custom-call | tf_op jit(solution)/shard_map/halo/pallas_call | solution.py:347
  140.4 1.8 pad_maximum_fusion
  142.2 4.3 %fusion.18 = f32[2048,512]{1,0:T(8,128)} fusion(bf16[2048,512]{1,0:T(8,128)(2,1)S(1)} %copy-done.2, bf16[256,512]{1,0:T(8,128)(2,1)S(1)} %get-tuple-element.18, bf16[9,512,512]{2,1,0:T(8,128)(2,1)} %param.20), kind=kOutput, calls=%fused_computation.30 | convolution fusion | flops 1077936128 | bytes 7077888 | tf_op jit(solution)/shard_map/dot_general | solution.py:31
  146.5 4.3 %fusion.16 = f32[2048,512]{1,0:T(8,128)} fusion(bf16[256,512]{1,0:T(8,128)(2,1)S(1)} %get-tuple-element.19, bf16[2048,512]{1,0:T(8,128)(2,1)S(1)} %copy-done.2, bf16[9,512,512]{2,1,0:T(8,128)(2,1)} %param.20), kind=kOutput, calls=%fused_computation.27 | convolution fusion | flops 1077936128 | bytes 7077888 | tf_op jit(solution)/shard_map/dot_general | solution.py:31
  150.8 2.3 %fusion.30 = f32[2048,512]{1,0:T(8,128)S(1)} fusion(bf16[2048,512]{1,0:T(8,128)(2,1)S(1)} %copy-done.2, bf16[9,512,512]{2,1,0:T(8,128)(2,1)} %param.20), kind=kOutput, calls=%fused_computation.40 | convolution fusion | flops 1073741824 | bytes 6815744 | tf_op jit(solution)/shard_map/dot_general | solution.py:31
  153.1 4.0 %pad_maximum_fusion.1 = (bf16[8,256,512]{2,1,0:T(8,128)(2,1)S(1)}, bf16[8,256,512]{2,1,0:T(8,128)(2,1)S(1)}, bf16[8,256,512]{2,1,0:T(8,128)(2,1)S(1)}, bf16[8,25...) fusion(bf16[10,1,512]{2,1,0:T(2,128)(2,1)S(1)} %copy.15, ...), kind=kLoop, calls=%fused_computation.25 | loop fusion | flops 12582912 | bytes 15214592 | tf_op jit(solution)/shard_map/concatenate | solution.py:456
  157.2 4.3 %fusion.34 = f32[2048,512]{1,0:T(8,128)} fusion(bf16[2048,512]{1,0:T(8,128)(2,1)S(1)} %bitcast.68, bf16[9,512,512]{2,1,0:T(8,128)(2,1)} %param.20), kind=kOutput, calls=%fused_computation.44 | convolution fusion | flops 1073741824 | bytes 6815744 | tf_op jit(solution)/shard_map/dot_general | solution.py:31
  161.5 4.3 %fusion.28 = f32[2048,512]{1,0:T(8,128)} fusion(bf16[2048,512]{1,0:T(8,128)(2,1)S(1)} %bitcast.67, bf16[9,512,512]{2,1,0:T(8,128)(2,1)} %param.20), kind=kOutput, calls=%fused_computation.38 | convolution fusion | flops 1073741824 | bytes 6815744 | tf_op jit(solution)/shard_map/dot_general | solution.py:31
  165.8 4.3 %fusion.32 = f32[2048,512]{1,0:T(8,128)} fusion(bf16[2048,512]{1,0:T(8,128)(2,1)S(1)} %bitcast.66, bf16[9,512,512]{2,1,0:T(8,128)(2,1)} %param.20), kind=kOutput, calls=%fused_computation.42 | convolution fusion | flops 1073741824 | bytes 6815744 | tf_op jit(solution)/shard_map/dot_general | solution.py:31
  170.0 4.3 %fusion.26 = f32[2048,512]{1,0:T(8,128)} fusion(bf16[2048,512]{1,0:T(8,128)(2,1)S(1)} %bitcast.65, bf16[9,512,512]{2,1,0:T(8,128)(2,1)} %param.20), kind=kOutput, calls=%fused_computation.36 | convolution fusion | flops 1073741824 | bytes 6815744 | tf_op jit(solution)/shard_map/dot_general | solution.py:31
  174.3 4.3 %fusion.37 = f32[2048,512]{1,0:T(8,128)} fusion(bf16[2048,512]{1,0:T(8,128)(2,1)S(1)} %bitcast.64, bf16[9,512,512]{2,1,0:T(8,128)(2,1)} %param.20), kind=kOutput, calls=%fused_computation.47 | convolution fusion | flops 1073741824 | bytes 6815744 | tf_op jit(solution)/shard_map/dot_general | solution.py:31
  178.6 12.5 %multiply_reduce_fusion = (f32[2048]{0:T(1024)S(1)}, f32[2048,512]{1,0:T(8,128)}) fusion(bf16[2048,512]{1,0:T(8,128)(2,1)S(1)} %bitcast.70, bf16[9,512,512]{2,1,0:T(8,128)(2,1)} %param.20, f32[2048,512]{1,0:T(8,128)} %fusion.16, f32[2048,512]{1,0:T(8,128)} %fusion.26, f32[2048,512]{1,0:T(8,128)} %fusion.28, f32[2048,512]{1,0:T(8,128)S(1)} %fusion.30, ...), kind=kOutput, calls=%fused_computation.12 | convolution fusion | flops 1086322688 | bytes 42475520 | tf_op jit(solution)/shard_map/dot_general | solution.py:31
  191.1 0.0 copy-done
  191.1 0.0 copy-done.11
  191.1 14.1 %add_convert_fusion = bf16[2048,512]{1,0:T(8,128)(2,1)} fusion(f32[2048,512]{1,0:T(8,128)} %get-tuple-element.28, bf16[2048,512]{1,0:T(8,128)(2,1)S(1)} %copy-done, bf16[512,2048]{1,0:T(8,128)(2,1)} %param.22, f32[512]{0:T(512)S(1)} %copy-done.11, f32[2048]{0:T(1024)S(1)} %add_rsqrt_fusion), kind=kOutput, calls=%fused_computation.10 | convolution fusion | flops 8632926208 | bytes 10496000 | tf_op jit(solution)/shard_map/dot_general | solution.py:31
  (14 shorter events, 0.0 us)
Async XLA Ops:
  0.0 191.1 %copy-start = (bf16[2048,512]{1,0:T(8,128)(2,1)S(1)}, bf16[2048,512]{1,0:T(8,128)(2,1)}, u32[]{:S(2)}) copy-start(bf16[2048,512]{1,0:T(8,128)(2,1)} %param.23) | copy-start | bytes 6291460
  0.0 0.9 copy-start.6
  0.9 0.7 copy-start.7
  3.6 21.7 %all-to-all-start.1 = ((s32[128,1,128]{2,1,0:T(1,128)}), s32[128,1,128]{2,1,0:T(1,128)S(1)}, u32[]{:S(2)}, u32[]{:S(2)}) async-start(s32[128,1,128]{2,1,0:T(1,128)} %bitcast.3), calls=%async_computation.1 | async-start | bytes 131072 | tf_op jit(solution)/shard_map/all_to_all | solution.py:492
  14.7 1.1 copy-start.4
  15.9 60.9 %copy-start.5 = (bf16[128,512]{1,0:T(8,128)(2,1)S(1)}, bf16[128,512]{1,0:T(8,128)(2,1)}, u32[]{:S(2)}) copy-start(bf16[128,512]{1,0:T(8,128)(2,1)} %weight.1) | copy-start | bytes 393220
  15.9 60.9 %copy-start.8 = (f32[512]{0:T(512)S(1)}, f32[512]{0:T(512)}, u32[]{:S(2)}) copy-start(f32[512]{0:T(512)} %param.17) | copy-start | bytes 6148
  15.9 60.9 %copy-start.9 = (f32[512]{0:T(512)S(1)}, f32[512]{0:T(512)}, u32[]{:S(2)}) copy-start(f32[512]{0:T(512)} %param.18) | copy-start | bytes 6148
  15.9 60.9 %copy-start.10 = (f32[512]{0:T(512)S(1)}, f32[512]{0:T(512)}, u32[]{:S(2)}) copy-start(f32[512]{0:T(512)} %param.19) | copy-start | bytes 6148
  23.6 1.7 copy-start.3
  127.2 1.6 copy-start.1
  128.8 13.4 %copy-start.2 = (bf16[2048,512]{1,0:T(8,128)(2,1)S(1)}, bf16[2048,512]{1,0:T(8,128)(2,1)}, u32[]{:S(2)}) copy-start(bf16[2048,512]{1,0:T(8,128)(2,1)} %get-tuple-element.17.normed) | copy-start | bytes 6291460
  178.6 12.5 %copy-start.11 = (f32[512]{0:T(512)S(1)}, f32[512]{0:T(512)}, u32[]{:S(2)}) copy-start(f32[512]{0:T(512)} %param.21) | copy-start | bytes 6148

commit v2 on v1

--- a/solution.py
+++ b/solution.py
@@ -104,7 +104,7 @@
         ),
         in_specs=[vmem] * 2,
         out_specs=[vmem] * 3,
-        compiler_params=pltpu.CompilerParams(vmem_limit_bytes=40 * MIB),
+        compiler_params=pltpu.CompilerParams(vmem_limit_bytes=16 * MIB),
         name="rank",
     )(dest, cell)
     send = pl.pallas_call(
@@ -113,7 +113,7 @@
         in_specs=[pl.BlockSpec(memory_space=pltpu.SMEM), vmem, vmem],
         out_specs=vmem,
         scratch_shapes=[pltpu.VMEM((rows + 2 * capacity, width), F32)],
-        compiler_params=pltpu.CompilerParams(vmem_limit_bytes=40 * MIB),
+        compiler_params=pltpu.CompilerParams(vmem_limit_bytes=16 * MIB),
         name="cut",
     )(starts, rank, feat)
     return send, cells
@@ -204,7 +204,7 @@
             pltpu.VMEM((cell_count, 128), F32),
             pltpu.VMEM((parts, sources // 8, 128), I32),
         ],
-        compiler_params=pltpu.CompilerParams(vmem_limit_bytes=50 * MIB),
+        compiler_params=pltpu.CompilerParams(vmem_limit_bytes=24 * MIB),
         name="assimilate",
     )(arrived, cells, state, weight, bias, obs_gain, norm_gain)
 
@@ -369,18 +369,19 @@
             pltpu.SemaphoreType.DMA,
         ],
         compiler_params=pltpu.CompilerParams(
-            collective_id=1, has_side_effects=True, vmem_limit_bytes=30 * MIB
+            collective_id=1, has_side_effects=True, vmem_limit_bytes=16 * MIB
         ),
         name="halo",
     )(normed)
 
 
-def block_kernel(
-    normed, north, south, seam, grid, conv_weight, mlp_gain, mlp_in, mlp_out, out, planes, *, per
+def encode_kernel(
+    normed, north, south, seam, grid, conv_weight, mlp_gain, mlp_in, mlp_out, out, planes
 ):
-    step = pl.program_id(0)
-    steps = pl.num_programs(0)
     side, width = north.shape
+    cells = normed.shape[0]
+    rows = cells // side
+    per = 2
     hidden_step = 512
 
     def put(row, values):
@@ -388,82 +389,54 @@
         at = lax.broadcasted_iota(I32, (side, width), 0)
         left = jnp.where(at == 0, 0.0, pltpu.roll(values, 1, 0))
         right = jnp.where(at == side - 1, seam[pl.ds(row, 1), :], pltpu.roll(values, side - 1, 0))
-        planes[row, :, 0:width] = left.astype(BF16)
-        planes[row, :, width : 2 * width] = values.astype(BF16)
-        planes[row, :, 2 * width : 3 * width] = right.astype(BF16)
-
-    def strip_row(row):
-        return normed[pl.ds(pl.multiple_of(row * side, side), side), :]
-
-    @pl.when(step == 0)
-    def _():
-        put(0, north[...])
-        put(1, normed[0:side, :])
-
-    for ahead in range(per):
-        row = step * per + 2 + ahead
-        if ahead < per - 1:
-            put(row, strip_row(row - 1))
-        else:
-            inner = strip_row(jnp.minimum(row - 1, steps * per - 1))
-            put(row, jnp.where(step == steps - 1, south[...], inner))
-
-    conv = None
-    for tap in range(3):
-        window = planes[pl.ds(step * per + tap, per)].reshape(per * side, 3 * width)
-        term = dot(window, conv_weight[tap])
-        conv = term if conv is None else conv + term
-    mid = grid[...].astype(F32) + conv
-    scale = lax.rsqrt(jnp.mean(mid * mid, axis=1, keepdims=True) + EPS)
-    normed_two = (mid * scale * mlp_gain[...]).astype(BF16)
-    result = mid
-    for part in range(mlp_in.shape[1] // hidden_step):
-        at = slice(part * hidden_step, (part + 1) * hidden_step)
-        hidden = gelu(dot(normed_two, mlp_in[:, at])).astype(BF16)
-        result = result + dot(hidden, mlp_out[at, :])
-    out[...] = result.astype(BF16)
-
-
-def encode(normed, north, south, seam, grid, conv_weight, mlp_gain, mlp_in, mlp_out, per=2):
+        to = pl.ds(pl.multiple_of(row * side, side), side)
+        planes[to, 0:width] = left.astype(BF16)
+        planes[to, width : 2 * width] = values.astype(BF16)
+        planes[to, 2 * width : 3 * width] = right.astype(BF16)
+
+    put(0, north[...])
+    put(rows + 1, south[...])
+
+    def inner(row, _):
+        put(row + 1, normed[pl.ds(pl.multiple_of(row * side, side), side), :])
+        return 0
+
+    lax.fori_loop(0, rows, inner, 0)
+
+    def one(step, _):
+        first = pl.multiple_of(step * (per * side), per * side)
+        conv = None
+        for tap in range(3):
+            window = planes[pl.ds(pl.multiple_of(first + tap * side, side), per * side), :]
+            term = dot(window, conv_weight[tap])
+            conv = term if conv is None else conv + term
+        mid = grid[pl.ds(first, per * side), :].astype(F32) + conv
+        scale = lax.rsqrt(jnp.mean(mid * mid, axis=1, keepdims=True) + EPS)
+        normed_two = (mid * scale * mlp_gain[...]).astype(BF16)
+        result = mid
+        for part in range(mlp_in.shape[1] // hidden_step):
+            at = slice(part * hidden_step, (part + 1) * hidden_step)
+            hidden = gelu(dot(normed_two, mlp_in[:, at])).astype(BF16)
+            result = result + dot(hidden, mlp_out[at, :])
+        out[pl.ds(first, per * side), :] = result.astype(BF16)
+        return 0
+
+    lax.fori_loop(0, rows // per, one, 0)
+
+
+def encode(normed, north, south, seam, grid, conv_weight, mlp_gain, mlp_in, mlp_out):
     cell_count, width = normed.shape
     side = north.shape[0]
-    rows = cell_count // side
-    whole = pl.BlockSpec(memory_space=pltpu.VMEM)
-    strip = pl.BlockSpec((per * side, width), lambda i: (i, 0))
-
-    def body(*refs):
-        block_kernel(*refs, per=per)
-
+    vmem = pl.BlockSpec(memory_space=pltpu.VMEM)
     return pl.pallas_call(
-        body,
-        grid=(rows // per,),
+        encode_kernel,
         out_shape=jax.ShapeDtypeStruct(normed.shape, BF16),
-        in_specs=[whole, whole, whole, whole, strip, whole, whole, whole, whole],
-        out_specs=strip,
-        scratch_shapes=[pltpu.VMEM((rows + 2, side, 3 * width), BF16)],
-        compiler_params=pltpu.CompilerParams(vmem_limit_bytes=56 * MIB),
+        in_specs=[vmem] * 9,
+        out_specs=vmem,
+        scratch_shapes=[pltpu.VMEM((cell_count + 2 * side, 3 * width), BF16)],
+        compiler_params=pltpu.CompilerParams(vmem_limit_bytes=40 * MIB),
         name="encode",
     )(normed, north, south, seam, grid, conv_weight, mlp_gain, mlp_in, mlp_out)
-
-
-def encode_plain(normed, north, south, seam, grid, conv_weight, mlp_gain, mlp_in, mlp_out):
-    cell_count, width = normed.shape
-    side = north.shape[0]
-    rows = cell_count // side
-    sides = jnp.concatenate([north, normed, south]).reshape(rows + 2, side, width)
-    zero_col = jnp.zeros((rows + 2, 1, width), BF16)
-    seam = seam[: rows + 2, None].astype(BF16)
-    padded = jnp.concatenate([zero_col, sides, seam], axis=1)
-    conv = jnp.zeros((cell_count, width), F32)
-    for tap_row in range(3):
-        for tap_col in range(3):
-            window = padded[tap_row : tap_row + rows, tap_col : tap_col + side].reshape(-1, width)
-            conv = conv + dot(window, conv_weight[3 * tap_row + tap_col])
-    mid = grid.astype(F32) + conv
-    scale = lax.rsqrt(jnp.mean(mid * mid, axis=-1, keepdims=True) + EPS)
-    normed_two = (mid * scale * mlp_gain).astype(BF16)
-    hidden = jax.nn.gelu(dot(normed_two, mlp_in)).astype(BF16)
-    return (mid + dot(hidden, mlp_out)).astype(BF16)
 
 
 def shards(
@@ -500,13 +473,13 @@
         norm_gain.reshape(1, width),
     )
     north, south, seam = exchange_halo(normed, tiles, rows)
-    result = encode_plain(
+    result = encode(
         normed,
         north,
         south,
         seam,
         grid,
-        conv_weight,
+        conv_weight.reshape(3, 3 * width, width),
         mlp_gain.reshape(1, width),
         mlp_in,
         mlp_out,

time: 206 us -> 158 us (0.77)
  matrix products: 58.9 us -> 0 us
  Pallas kernels: 71.8 us -> 92.6 us
  other arithmetic: 5.82 us -> 0.01 us
  local copies, waits for them, and re-layouts: 5.98 us -> 2.6 us
    dot_general x10 -> x0, matrix products: 58.9 us -> none  [dot(): return jnp.dot(a, b, preferred_element_type=F32)]
    pallas_call x0 -> x1, Pallas kernels: none -> 24.6 us  [encode(): pl.pallas_call(encode_kernel, out_shape=jax.ShapeDtypeStruct(normed.shape...]
    concatenate x2 -> x0, other arithmetic: 5.81 us -> none  [the longest x1 4.05 us: encode_plain(): padded = jnp.concatenate([zero_col, sides, seam], axis=1)]
    pallas_call x1, Pallas kernels: 50.4 us -> 46.5 us  [assimilate(): pl.pallas_call(assimilate_kernel, out_shape=(jax.ShapeDtypeStruct(state.s...]
    unnamed x24 -> x26, local copies, waits for them, and re-layouts: 5.96 us -> 2.6 us
  transfers between devices with their start and end apart: 1 -> 1, of which waited for: 0 -> 1; matrix products, arithmetic and copies ran while one was open for 0% -> 0% of each run, Pallas kernels for 4% -> 5%
where the time goes in v2:
time: 158 us
  Pallas kernels  92.6 us (59%)
  blocking collectives  50.9 us (32%)
  starting transfers between devices  11.1 us (7%)
  local copies, waits for them, and re-layouts  2.6 us (2%)
    all_to_all x1, blocking collectives, shards(): lax.all_to_all(send, ('face', 'tile'), split_axis=0, concat_axis=0, tiled...  50.9 us
    pallas_call x1, Pallas kernels, assimilate(): pl.pallas_call(assimilate_kernel, out_shape=(jax.ShapeDtypeStruct(state.s...  46.5 us
    pallas_call x1, Pallas kernels, encode(): pl.pallas_call(encode_kernel, out_shape=jax.ShapeDtypeStruct(normed.shape...  24.6 us
    pallas_call x1, Pallas kernels, exchange_halo(): pl.pallas_call(halo_kernel, out_shape=(jax.ShapeDtypeStruct((side, width)...  11.8 us
    all_to_all x1, starting transfers between devices, shards(): lax.all_to_all(cells, ('face', 'tile'), split_axis=0, concat_axis=0, tile...  11.1 us
    pallas_call x1, Pallas kernels, pack(): pl.pallas_call(cut_kernel, out_shape=jax.ShapeDtypeStruct((devices, capac...  7.73 us
  transfers between devices with their start and end apart: 1, of which 1 were waited for; matrix products, arithmetic and copies ran while one was open for 0% of the time, Pallas kernels for 5%

profile of v2, /device:TPU:0, one launch (start us, length us, event | category | flops | bytes accessed | tf_op | source)
XLA Modules:
  0.0 157.8 jit_solution(67332533084263646)
XLA Ops:
  0.0 0.0 copy-start.5
  0.0 0.7 copy-done.5
  0.7 0.7 copy-done.6
  1.4 2.0 %rank.1 = (s32[1,3072]{1,0:T(1,128)S(1)}, s32[1,128]{1,0:T(1,128)S(1)}, s32[128,128]{1,0:T(8,128)}) custom-call(s32[1,3072]{1,0:T(1,128)S(1)} %bitcast.18, s32[1,3072]{1,0:T(1,128)S(1)} %bitcast.19), custom_call_target="tpu_custom_call" | custom-call | tf_op jit(solution)/shard_map/rank/pallas_call | solution.py:98
  3.4 11.1 %all-to-all-start.1 = ((s32[128,1,128]{2,1,0:T(1,128)}), s32[128,1,128]{2,1,0:T(1,128)S(1)}, u32[]{:S(2)}, u32[]{:S(2)}) async-start(s32[128,1,128]{2,1,0:T(1,128)} %bitcast.3), calls=%async_computation.1 | async-start | bytes 131072 | tf_op jit(solution)/shard_map/all_to_all | solution.py:465
  14.6 0.0 copy-start.3
  14.6 1.1 copy-done.3
  15.7 0.0 copy-start.4
  15.7 7.7 %cut.1 = bf16[128,6,16,128]{3,2,1,0:T(8,128)(2,1)S(1)} custom-call(s32[1,128]{1,0:T(1,128)S(1)} %get-tuple-element.13.starts, s32[1,3072]{1,0:T(1,128)S(1)} %get-tuple-element.14.rank, bf16[3072,128]{1,0:T(8,128)(2,1)S(1)} %copy-done.3), custom_call_target="tpu_custom_call" | custom-call | tf_op jit(solution)/shard_map/cut/pallas_call | solution.py:110
  23.5 0.0 copy-start.7
  23.5 0.0 copy-start.8
  23.5 0.0 copy-start.9
  23.5 0.3 all-to-all-done.1
  23.8 0.0 copy-start.2
  23.8 50.9 %all_to_all.16.arrived = bf16[128,6,16,128]{3,2,1,0:T(8,128)(2,1)S(1)} all-to-all(bf16[128,6,16,128]{3,2,1,0:T(8,128)(2,1)S(1)} %cut.1), channel_id=1, replica_groups=mesh['face'=4,'tile'=32] {'face','tile'}, dimensions={0} | all-to-all | bytes 6291456 | tf_op jit(solution)/shard_map/all_to_all | solution.py:464
  74.7 0.0 copy-done.4
  74.7 0.0 copy-done.7
  74.7 0.0 copy-done.8
  74.8 0.0 copy-done.9
  74.8 0.0 copy-done.2
  74.8 0.0 slice-start.1
  74.8 0.0 copy-start.1
  74.8 46.5 %assimilate.1 = (bf16[2048,512]{1,0:T(8,128)(2,1)S(1)}, bf16[2048,512]{1,0:T(8,128)(2,1)S(1)}) custom-call(bf16[128,6,16,128]{3,2,1,0:T(8,128)(2,1)S(1)} %all_to_all.16.arrived, s32[128,128]{1,0:T(8,128)S(1)} %bitcast.17, bf16[2048,512]{1,0:T(8,128)(2,1)S(1)} %bitcast.16, bf16[128,512]{1,0:T(8,128)(2,1)S(1)} %copy-done.4, f32[1,512]{1,0:T(1,128)S(1)} %bitcast.20, ...), custom_call_target="tpu_custom_call" | custom-call | tf_op jit(solution)/shard_map/assimilate/pallas_call | solution.py:196
  121.3 0.0 copy-start
  121.3 0.0 copy-start.10
  121.3 11.8 %halo.1 = (bf16[256,512]{1,0:T(8,128)(2,1)S(1)}, bf16[256,512]{1,0:T(8,128)(2,1)S(1)}, f32[16,512]{1,0:T(8,128)S(1)}) custom-call(bf16[2048,512]{1,0:T(8,128)(2,1)S(1)} %get-tuple-element.16.normed), custom_call_target="tpu_custom_call" | custom-call | tf_op jit(solution)/shard_map/halo/pallas_call | solution.py:347
  133.1 0.0 slice-done
  133.2 0.0 slice-done.1
  133.2 0.0 copy-done.1
  133.2 0.0 copy-done
  133.2 0.0 copy-done.10
  133.2 24.6 %encode.1 = bf16[2048,512]{1,0:T(8,128)(2,1)} custom-call(bf16[2048,512]{1,0:T(8,128)(2,1)S(1)} %get-tuple-element.16.normed, bf16[256,512]{1,0:T(8,128)(2,1)S(1)} %get-tuple-element.17.north, bf16[256,512]{1,0:T(8,128)(2,1)S(1)} %get-tuple-element.18.south, f32[16,512]{1,0:T(8,128)S(1)} %get-tuple-element.19.seam, ...), custom_call_target="tpu_custom_call" | custom-call | tf_op jit(solution)/shard_map/encode/pallas_call | solution.py:431
  (3 shorter events, 0.0 us)
Async XLA Ops:
  0.0 0.7 copy-start.5
  0.7 0.7 copy-start.6
  3.4 20.4 %all-to-all-start.1 = ((s32[128,1,128]{2,1,0:T(1,128)}), s32[128,1,128]{2,1,0:T(1,128)S(1)}, u32[]{:S(2)}, u32[]{:S(2)}) async-start(s32[128,1,128]{2,1,0:T(1,128)} %bitcast.3), calls=%async_computation.1 | async-start | bytes 131072 | tf_op jit(solution)/shard_map/all_to_all | solution.py:465
  14.6 1.1 copy-start.3
  15.7 59.0 %copy-start.4 = (bf16[128,512]{1,0:T(8,128)(2,1)S(1)}, bf16[128,512]{1,0:T(8,128)(2,1)}, u32[]{:S(2)}) copy-start(bf16[128,512]{1,0:T(8,128)(2,1)} %weight.1) | copy-start | bytes 393220
  23.5 51.3 %copy-start.7 = (f32[512]{0:T(512)S(1)}, f32[512]{0:T(512)}, u32[]{:S(2)}) copy-start(f32[512]{0:T(512)} %param.17) | copy-start | bytes 6148
  23.5 51.3 %copy-start.8 = (f32[512]{0:T(512)S(1)}, f32[512]{0:T(512)}, u32[]{:S(2)}) copy-start(f32[512]{0:T(512)} %param.18) | copy-start | bytes 6148
  23.5 51.2 %copy-start.9 = (f32[512]{0:T(512)S(1)}, f32[512]{0:T(512)}, u32[]{:S(2)}) copy-start(f32[512]{0:T(512)} %param.19) | copy-start | bytes 6148
  23.8 50.9 %copy-start.2 = (bf16[1,1,8,256,512]{4,3,2,1,0:T(8,128)(2,1)S(1)}, bf16[1,1,8,256,512]{4,3,2,1,0:T(8,128)(2,1)}, u32[]{:S(2)}) copy-start(bf16[1,1,8,256,512]{4,3,2,1,0:T(8,128)(2,1)} %param.12) | copy-start | bytes 6291460
  23.8 109.3 %slice-start = ((s8[4718592]{0:T(1024)(128)(4,1)}), s8[4194304]{0:T(1024)(128)(4,1)S(1)}, s32[]{:S(2)}) async-start(s8[4718592]{0:T(1024)(128)(4,1)} %bitcast.13), calls=%async_computation.2 | async-start | bytes 8388608
  74.8 58.4 %slice-start.1 = ((s8[4718592]{0:T(1024)(128)(4,1)}), s8[524288]{0:T(1024)(128)(4,1)S(1)}, s32[]{:S(2)}) async-start(s8[4718592]{0:T(1024)(128)(4,1)} %bitcast.13), calls=%async_computation.3 | async-start | bytes 1048576
  74.8 58.4 %copy-start.1 = (bf16[2048,512]{1,0:T(8,128)(2,1)S(1)}, bf16[2048,512]{1,0:T(8,128)(2,1)}, u32[]{:S(2)}) copy-start(bf16[2048,512]{1,0:T(8,128)(2,1)} %mlp_out.1) | copy-start | bytes 6291460
  121.3 11.9 %copy-start = (bf16[512,2048]{1,0:T(8,128)(2,1)S(1)}, bf16[512,2048]{1,0:T(8,128)(2,1)}, u32[]{:S(2)}) copy-start(bf16[512,2048]{1,0:T(8,128)(2,1)} %mlp_in.1) | copy-start | bytes 6291460
  121.3 11.9 %copy-start.10 = (f32[512]{0:T(512)S(1)}, f32[512]{0:T(512)}, u32[]{:S(2)}) copy-start(f32[512]{0:T(512)} %param.21) | copy-start | bytes 6148

commit v3 on v2

--- a/solution.py
+++ b/solution.py
@@ -69,9 +69,9 @@
 
 
 def cut_kernel(starts, rank, feat, send, ordered):
-    devices = send.shape[0]
+    parts, devices = send.shape[:2]
     rows = feat.shape[0]
-    capacity = send.shape[1] * send.shape[2]
+    capacity = parts * UNIT
 
     def sort_block(block, _):
         first = pl.multiple_of(block * BLOCK, BLOCK)
@@ -86,7 +86,9 @@
 
     def cut(target, _):
         values = ordered[pl.ds(starts[0, target], capacity), :]
-        send[target] = values.astype(BF16).reshape(send.shape[1:])
+        values = values.astype(BF16)
+        for part in range(parts):
+            send[part, target] = values[part * UNIT : (part + 1) * UNIT]
         return 0
 
     lax.fori_loop(0, devices, cut, 0, unroll=4)
@@ -109,7 +111,7 @@
     )(dest, cell)
     send = pl.pallas_call(
         cut_kernel,
-        out_shape=jax.ShapeDtypeStruct((devices, capacity // UNIT, UNIT, width), BF16),
+        out_shape=jax.ShapeDtypeStruct((capacity // UNIT, devices, UNIT, width), BF16),
         in_specs=[pl.BlockSpec(memory_space=pltpu.SMEM), vmem, vmem],
         out_specs=vmem,
         scratch_shapes=[pltpu.VMEM((rows + 2 * capacity, width), F32)],
@@ -135,31 +137,51 @@
     return jnp.sum(value, axis=1).astype(I32) - 1
 
 
+def match_rows(ids, row):
+    wide = jnp.broadcast_to(row, (UNIT, 128)).astype(BF16)
+    wide = jnp.concatenate([wide] * (128 // UNIT), axis=0)
+    return jnp.where(ids == wide, jnp.ones_like(ids), jnp.zeros_like(ids))
+
+
 def add_part(feats, spots, weight, bias, embed, total, count):
     slots = feats.shape[0]
     for block in range(slots // 512):
         at = slice(block * 512, (block + 1) * 512)
         embed[at, :] = gelu(dot(feats[at], weight[...]) + bias[...]).astype(BF16)
+    groups = slots // 128
+    ids = lax.broadcasted_iota(I32, (128, 128), 0).astype(F32).astype(BF16)
+    spot = spots[...]
+    high = lax.shift_right_arithmetic(spot, 7)
+    low = jnp.where(spot < 0, -1, spot - high * 128).astype(F32)
+    high_f = high.astype(F32)
+
+    def matches(rows):
+        return jnp.concatenate(
+            [match_rows(ids, rows[group : group + 1, :]) for group in range(groups)], axis=1
+        )
+
+    count[...] += dot_lanes(matches(low), matches(high_f))
+    per = 4
 
     def cell_block(block, _):
-        first = pl.multiple_of(block * BLOCK, BLOCK)
-        ids = lax.broadcasted_iota(I32, (BLOCK, 128), 0) + first
-        hits = [ones_where(ids == spots[group : group + 1, :]) for group in range(slots // 128)]
-        seen = hits[0]
-        for hit in hits[1:]:
-            seen = seen + hit
-        match = jnp.concatenate([hit.astype(BF16) for hit in hits], axis=1)
-        total[pl.ds(first, BLOCK), :] += dot(match, embed[...])
-        count[pl.ds(first, BLOCK), :] += seen
-        return 0
-
-    lax.fori_loop(0, total.shape[0] // BLOCK, cell_block, 0)
+        match = jnp.concatenate(
+            [matches(jnp.where(high == block * per + part, low, -1.0)) for part in range(per)],
+            axis=0,
+        )
+        at = pl.ds(pl.multiple_of(block * (per * 128), per * 128), per * 128)
+        total[at, :] += dot(match, embed[...])
+        return 0
+
+    lax.fori_loop(0, total.shape[0] // (per * 128), cell_block, 0)
 
 
 def finish_grid(state, obs_gain, norm_gain, total, count, grid, normed):
+    lane = lax.broadcasted_iota(I32, count.shape, 1)
+
     def block_of(block, _):
-        at = pl.ds(pl.multiple_of(block * BLOCK, BLOCK), BLOCK)
-        number = jnp.maximum(jnp.sum(count[at, :], axis=1, keepdims=True), 1.0)
+        at = pl.ds(pl.multiple_of(block * 128, 128), 128)
+        number = jnp.sum(jnp.where(lane == block, count[...], 0.0), axis=1, keepdims=True)
+        number = jnp.maximum(number, 1.0)
         value = state[at, :].astype(F32) + obs_gain[...] * (total[at, :] * (1.0 / number))
         rounded = value.astype(BF16)
         grid[at, :] = rounded
@@ -168,45 +190,160 @@
         normed[at, :] = (value * scale * norm_gain[...]).astype(BF16)
         return 0
 
-    lax.fori_loop(0, total.shape[0] // BLOCK, block_of, 0)
-
-
-def assimilate_kernel(
-    arrived, cells, state, weight, bias, obs_gain, norm_gain, grid, normed, embed, total, count, spots
+    lax.fori_loop(0, total.shape[0] // 128, block_of, 0)
+
+
+def gather_kernel(
+    send, cells, state, weight, bias, obs_gain, norm_gain, grid, normed,
+    held, cell_held, cell_flat, spots, embed, total, count,
+    send_sems, recv_sems, own_sems,
 ):
-    parts = arrived.shape[1]
-    sources = arrived.shape[0]
+    parts = send.shape[0]
+    face, tile = lax.axis_index("face"), lax.axis_index("tile")
+    sizes = send.shape[1:4]
+    mine = (face, tile // sizes[2], lax.rem(tile, sizes[2]))
+    barrier = pltpu.get_barrier_semaphore()
+
+    def other(dim, step):
+        place = list(mine)
+        place[dim] = lax.rem(mine[dim] + step, sizes[dim])
+        return place[dim], (place[0], place[1] * sizes[2] + place[2])
+
+    for dim in range(3):
+        def greet(step, _, dim=dim):
+            pl.semaphore_signal(
+                barrier, inc=1, device_id=other(dim, step)[1], device_id_type=MESH
+            )
+            return 0
+
+        lax.fori_loop(1, sizes[dim], greet, 0)
+
+    def dim_of(part, stage):
+        return (part + stage) % 3
+
+    def views(part, stage):
+        if part == parts:
+            source = cells if stage == 0 else cell_held.at[stage - 1]
+            return source, cell_held.at[stage]
+        source = send.at[part] if stage == 0 else held.at[stage - 1, part]
+        return source, held.at[stage, part]
+
+    def along(ref, dim, place):
+        return ref.at[(slice(None),) * dim + (place,)]
+
+    def copies(part, stage, step):
+        dim = dim_of(part, stage)
+        source, target = views(part, stage)
+        place, device = other(dim, step)
+        return pltpu.make_async_remote_copy(
+            src_ref=along(source, dim, place),
+            dst_ref=along(target, dim, mine[dim]),
+            send_sem=send_sems.at[part * 3 + stage, step],
+            recv_sem=recv_sems.at[part * 3 + stage, step],
+            device_id=device,
+            device_id_type=MESH,
+        )
+
+    def own(part, stage):
+        dim = dim_of(part, stage)
+        source, target = views(part, stage)
+        return pltpu.make_async_copy(
+            along(source, dim, mine[dim]), along(target, dim, mine[dim]),
+            own_sems.at[part * 3 + stage],
+        )
+
+    def start(part, stage):
+        def one(step, _):
+            copies(part, stage, step).start()
+            return 0
+
+        lax.fori_loop(1, sizes[dim_of(part, stage)], one, 0)
+        own(part, stage).start()
+
+    def finish(part, stage):
+        def one(step, _):
+            copies(part, stage, step).wait()
+            return 0
+
+        own(part, stage).wait()
+        lax.fori_loop(1, sizes[dim_of(part, stage)], one, 0)
+
+    def advance(which, stage):
+        for part in which:
+            finish(part, stage)
+            start(part, stage + 1)
+
+    def add(part, _=None):
+        feats = held[2, part].reshape(-1, send.shape[-1])
+        add_part(feats, spots.at[part], weight, bias, embed, total, count)
+        return 0
+
+    early, late = list(range(parts // 2)), list(range(parts // 2, parts))
+    pl.semaphore_wait(barrier, sum(sizes) - 3)
+    start(parts, 0)
+    for part in early:
+        start(part, 0)
+    for part in late:
+        start(part, 0)
     total[...] = jnp.zeros_like(total)
     count[...] = jnp.zeros_like(count)
+    advance([parts], 0)
+    advance(early, 0)
+    advance([parts], 1)
+    advance(early, 1)
+    advance(late, 0)
+    finish(parts, 2)
+
+    def lay(row, _):
+        across = sizes[1] * sizes[2]
+        cell_flat[pl.ds(row, 1), :] = cell_held[
+            2, row // across, lax.rem(row, across) // sizes[2], lax.rem(row, sizes[2])
+        ]
+        return 0
+
+    lax.fori_loop(0, cell_flat.shape[0], lay, 0)
     for part in range(parts):
-        spots[part] = spread_cells(cells[...], part)
-
-    def one(part, _):
-        feats = arrived[:, part].reshape(sources * UNIT, arrived.shape[3])
-        add_part(feats, spots.at[part], weight, bias, embed, total, count)
-        return 0
-
-    lax.fori_loop(0, parts, one, 0)
+        spots[part] = spread_cells(cell_flat[...], part)
+    finish(early[0], 2)
+    add(early[0])
+    advance(late, 1)
+    for part in early[1:]:
+        finish(part, 2)
+    lax.fori_loop(early[1], early[-1] + 1, add, 0)
+    for part in late:
+        finish(part, 2)
+    lax.fori_loop(late[0], late[-1] + 1, add, 0)
     finish_grid(state, obs_gain, norm_gain, total, count, grid, normed)
 
 
-def assimilate(arrived, cells, state, weight, bias, obs_gain, norm_gain):
+def assimilate(send, cells, state, weight, bias, obs_gain, norm_gain):
     cell_count, width = state.shape
-    sources, parts = arrived.shape[:2]
+    parts = send.shape[0]
+    sources = cells.shape[0] * cells.shape[1] * cells.shape[2]
+    vmem = pl.BlockSpec(memory_space=pltpu.VMEM)
+    longest = max(send.shape[1:4])
     return pl.pallas_call(
-        assimilate_kernel,
+        gather_kernel,
         out_shape=(jax.ShapeDtypeStruct(state.shape, BF16),) * 2,
-        in_specs=[pl.BlockSpec(memory_space=pltpu.VMEM)] * 7,
-        out_specs=[pl.BlockSpec(memory_space=pltpu.VMEM)] * 2,
+        in_specs=[vmem] * 7,
+        out_specs=[vmem] * 2,
         scratch_shapes=[
+            pltpu.VMEM((3,) + send.shape, BF16),
+            pltpu.VMEM((3,) + cells.shape, I32),
+            pltpu.VMEM((sources, 128), I32),
+            pltpu.VMEM((parts, sources // 8, 128), I32),
             pltpu.VMEM((sources * UNIT, width), BF16),
             pltpu.VMEM((cell_count, width), F32),
-            pltpu.VMEM((cell_count, 128), F32),
-            pltpu.VMEM((parts, sources // 8, 128), I32),
+            pltpu.VMEM((128, 128), F32),
+            pltpu.SemaphoreType.DMA((parts * 3 + 3, longest)),
+            pltpu.SemaphoreType.DMA((parts * 3 + 3, longest)),
+            pltpu.SemaphoreType.DMA((parts * 3 + 3,)),
         ],
-        compiler_params=pltpu.CompilerParams(vmem_limit_bytes=24 * MIB),
-        name="assimilate",
-    )(arrived, cells, state, weight, bias, obs_gain, norm_gain)
+        compiler_params=pltpu.CompilerParams(
+            collective_id=0, has_side_effects=True, vmem_limit_bytes=34 * MIB
+        ),
+        name="gather",
+    )(send, cells, state, weight, bias, obs_gain, norm_gain)
 
 
 def halo_kernel(
@@ -461,11 +598,11 @@
     send, cells = pack(
         obs_dest.reshape(1, held), obs_cell.reshape(1, held), obs_feat, devices, capacity
     )
-    arrived = lax.all_to_all(send, ("face", "tile"), split_axis=0, concat_axis=0, tiled=True)
-    cells = lax.all_to_all(cells, ("face", "tile"), split_axis=0, concat_axis=0, tiled=True)
+    faces = lax.axis_size("face")
+    across = (faces, 4, tiles // 4)
     grid, normed = assimilate(
-        arrived,
-        cells,
+        send.reshape(send.shape[:1] + across + send.shape[2:]),
+        cells.reshape(across + (1, 128)),
         state.reshape(rows * side, width),
         obs_weight,
         obs_bias.reshape(1, width),

time: 158 us -> 134 us (0.85)
  blocking collectives: 50.9 us -> 0 us
  Pallas kernels: 92.6 us -> 128 us
  starting transfers between devices: 11.1 us -> 0 us
  local copies, waits for them, and re-layouts: 2.6 us -> 5.66 us
    all_to_all x1 -> x0, blocking collectives: 50.9 us -> none  [shards(): lax.all_to_all(send, ('face', 'tile'), split_axis=0, concat_axis=0, tiled...]
    pallas_call x2, Pallas kernels: 54.2 us -> 90.3 us  [the longest x1 82.5 us: assimilate(): pl.pallas_call(gather_kernel, out_shape=(jax.ShapeDtypeStruct(state.shape...]
    all_to_all x1 -> x0, starting transfers between devices: 11.1 us -> none  [shards(): lax.all_to_all(cells, ('face', 'tile'), split_axis=0, concat_axis=0, tile...]
    unnamed x26, local copies, waits for them, and re-layouts: 2.6 us -> 5.66 us
  transfers between devices with their start and end apart: 1 -> 0, of which waited for: 1 -> 0; matrix products, arithmetic and copies ran while one was open for 0% -> 0% of each run, Pallas kernels for 5% -> 0%
where the time goes in v3:
time: 134 us
  Pallas kernels  128 us (96%)
  local copies, waits for them, and re-layouts  5.66 us (4%)
    pallas_call x1, Pallas kernels, assimilate(): pl.pallas_call(gather_kernel, out_shape=(jax.ShapeDtypeStruct(state.shape...  82.5 us
    pallas_call x1, Pallas kernels, encode(): pl.pallas_call(encode_kernel, out_shape=jax.ShapeDtypeStruct(normed.shape...  24.6 us
    pallas_call x1, Pallas kernels, exchange_halo(): pl.pallas_call(halo_kernel, out_shape=(jax.ShapeDtypeStruct((side, width)...  12 us
    pallas_call x1, Pallas kernels, pack(): pl.pallas_call(cut_kernel, out_shape=jax.ShapeDtypeStruct((capacity // UN...  7.78 us
    unnamed x26, local copies, waits for them, and re-layouts  5.66 us

profile of v3, /device:TPU:0, one launch (start us, length us, event | category | flops | bytes accessed | tf_op | source)
XLA Modules:
  0.0 134.0 jit_solution(10622395516201476506)
XLA Ops:
  0.0 0.0 copy-start.2
  0.0 0.0 copy-start.5
  0.0 0.9 copy-done.5
  0.9 0.0 copy-start.6
  0.9 0.7 copy-done.6
  1.6 1.4 %rank.1 = (s32[1,3072]{1,0:T(1,128)S(1)}, s32[1,128]{1,0:T(1,128)S(1)}, s32[128,128]{1,0:T(8,128)S(1)}) custom-call(s32[1,3072]{1,0:T(1,128)S(1)} %bitcast.17, s32[1,3072]{1,0:T(1,128)S(1)} %bitcast.18), custom_call_target="tpu_custom_call" | custom-call | tf_op jit(solution)/shard_map/rank/pallas_call | solution.py:100
  3.0 0.0 copy-start.3
  3.0 1.1 copy-done.3
  4.1 0.0 slice-start
  4.1 7.8 %cut.1 = bf16[6,128,16,128]{3,2,1,0:T(8,128)(2,1)S(1)} custom-call(s32[1,128]{1,0:T(1,128)S(1)} %get-tuple-element.13.starts, s32[1,3072]{1,0:T(1,128)S(1)} %get-tuple-element.14.rank, bf16[3072,128]{1,0:T(8,128)(2,1)S(1)} %copy-done.3), custom_call_target="tpu_custom_call" | custom-call | tf_op jit(solution)/shard_map/cut/pallas_call | solution.py:112
  11.9 0.0 copy-done.2
  11.9 0.0 copy-start.4
  11.9 0.9 copy-done.4
  12.8 0.0 copy-start.7
  12.8 0.7 copy-done.7
  13.5 0.0 copy-start.8
  13.5 0.7 copy-done.8
  14.2 0.0 copy-start.9
  14.2 0.7 copy-done.9
  14.9 0.0 slice-start.1
  14.9 0.0 copy-start.1
  14.9 82.5 %gather.1 = (bf16[2048,512]{1,0:T(8,128)(2,1)S(1)}, bf16[2048,512]{1,0:T(8,128)(2,1)S(1)}) custom-call(bf16[6,4,4,8,16,128]{5,4,3,2,1,0:T(8,128)(2,1)S(1)} %bitcast.11, s32[4,4,8,1,128]{4,3,2,1,0:T(1,128)S(1)} %bitcast.16, bf16[2048,512]{1,0:T(8,128)(2,1)S(1)} %bitcast.15, bf16[128,512]{1,0:T(8,128)(2,1)S(1)} %copy-done.4, f32[1,512]{1,0:T(1,128)S(1)} %bitcast.19, ...), custom_call_target="tpu_custom_call" | custom-call | tf_op jit(solution)/shard_map/gather/pallas_call | solution.py:325
  97.3 0.0 copy-start
  97.4 0.0 copy-start.10
  97.4 12.0 %halo.1 = (bf16[256,512]{1,0:T(8,128)(2,1)S(1)}, bf16[256,512]{1,0:T(8,128)(2,1)S(1)}, f32[16,512]{1,0:T(8,128)S(1)}) custom-call(bf16[2048,512]{1,0:T(8,128)(2,1)S(1)} %get-tuple-element.16.normed), custom_call_target="tpu_custom_call" | custom-call | tf_op jit(solution)/shard_map/halo/pallas_call | solution.py:484
  109.4 0.0 slice-done
  109.4 0.0 slice-done.1
  109.4 0.0 copy-done.1
  109.4 0.0 copy-done
  109.4 0.0 copy-done.10
  109.4 24.6 %encode.1 = bf16[2048,512]{1,0:T(8,128)(2,1)} custom-call(bf16[2048,512]{1,0:T(8,128)(2,1)S(1)} %get-tuple-element.16.normed, bf16[256,512]{1,0:T(8,128)(2,1)S(1)} %get-tuple-element.17.north, bf16[256,512]{1,0:T(8,128)(2,1)S(1)} %get-tuple-element.18.south, f32[16,512]{1,0:T(8,128)S(1)} %get-tuple-element.19.seam, ...), custom_call_target="tpu_custom_call" | custom-call | tf_op jit(solution)/shard_map/encode/pallas_call | solution.py:568
  (1 shorter events, 0.0 us)
Async XLA Ops:
  0.0 11.9 %copy-start.2 = (bf16[1,1,8,256,512]{4,3,2,1,0:T(8,128)(2,1)S(1)}, bf16[1,1,8,256,512]{4,3,2,1,0:T(8,128)(2,1)}, u32[]{:S(2)}) copy-start(bf16[1,1,8,256,512]{4,3,2,1,0:T(8,128)(2,1)} %param.12) | copy-start | bytes 6291460
  0.0 0.9 copy-start.5
  0.9 0.7 copy-start.6
  3.0 1.1 copy-start.3
  4.1 105.3 %slice-start = ((s8[4718592]{0:T(1024)(128)(4,1)}), s8[4194304]{0:T(1024)(128)(4,1)S(1)}, s32[]{:S(2)}) async-start(s8[4718592]{0:T(1024)(128)(4,1)} %bitcast.12), calls=%async_computation | async-start | bytes 8388608
  11.9 0.9 copy-start.4
  12.8 0.7 copy-start.7
  13.5 0.7 copy-start.8
  14.2 0.7 copy-start.9
  14.9 94.5 %slice-start.1 = ((s8[4718592]{0:T(1024)(128)(4,1)}), s8[524288]{0:T(1024)(128)(4,1)S(1)}, s32[]{:S(2)}) async-start(s8[4718592]{0:T(1024)(128)(4,1)} %bitcast.12), calls=%async_computation.1 | async-start | bytes 1048576
  14.9 94.5 %copy-start.1 = (bf16[2048,512]{1,0:T(8,128)(2,1)S(1)}, bf16[2048,512]{1,0:T(8,128)(2,1)}, u32[]{:S(2)}) copy-start(bf16[2048,512]{1,0:T(8,128)(2,1)} %mlp_out.1) | copy-start | bytes 6291460
  97.3 12.0 %copy-start = (bf16[512,2048]{1,0:T(8,128)(2,1)S(1)}, bf16[512,2048]{1,0:T(8,128)(2,1)}, u32[]{:S(2)}) copy-start(bf16[512,2048]{1,0:T(8,128)(2,1)} %mlp_in.1) | copy-start | bytes 6291460
  97.4 12.0 %copy-start.10 = (f32[512]{0:T(512)S(1)}, f32[512]{0:T(512)}, u32[]{:S(2)}) copy-start(f32[512]{0:T(512)} %param.21) | copy-start | bytes 6148

commit v4 on v3

--- a/solution.py
+++ b/solution.py
@@ -20,6 +20,14 @@
 def gelu(x):
     inner = x * (math.sqrt(2.0 / math.pi) + (0.044715 * math.sqrt(2.0 / math.pi)) * (x * x))
     half = 0.5 * x
+    return half + half * jnp.tanh(inner)
+
+
+def gelu_narrow(x):
+    x = x.astype(BF16)
+    slope = BF16(math.sqrt(2.0 / math.pi))
+    inner = x * (slope + BF16(0.044715 * math.sqrt(2.0 / math.pi)) * (x * x))
+    half = BF16(0.5) * x
     return half + half * jnp.tanh(inner)
 
 
@@ -143,27 +151,30 @@
     return jnp.where(ids == wide, jnp.ones_like(ids), jnp.zeros_like(ids))
 
 
-def add_part(feats, spots, weight, bias, embed, total, count):
-    slots = feats.shape[0]
-    for block in range(slots // 512):
-        at = slice(block * 512, (block + 1) * 512)
-        embed[at, :] = gelu(dot(feats[at], weight[...]) + bias[...]).astype(BF16)
-    groups = slots // 128
+def embed_block(feats, block, weight, bias, embed):
+    at = pl.ds(pl.multiple_of(block * 512, 512), 512)
+    rows = feats[pl.ds(block * (512 // UNIT), 512 // UNIT)].reshape(512, feats.shape[-1])
+    embed[at, :] = gelu_narrow(dot(rows, weight[...]) + bias[...])
+
+
+def add_part(spots, embed, total, count, beside):
+    groups = spots.shape[0]
     ids = lax.broadcasted_iota(I32, (128, 128), 0).astype(F32).astype(BF16)
     spot = spots[...]
     high = lax.shift_right_arithmetic(spot, 7)
     low = jnp.where(spot < 0, -1, spot - high * 128).astype(F32)
-    high_f = high.astype(F32)
 
     def matches(rows):
         return jnp.concatenate(
             [match_rows(ids, rows[group : group + 1, :]) for group in range(groups)], axis=1
         )
 
-    count[...] += dot_lanes(matches(low), matches(high_f))
-    per = 4
+    count[...] += dot_lanes(matches(low), matches(high.astype(F32)))
+    per = 8
 
     def cell_block(block, _):
+        beside(2 * block)
+        beside(2 * block + 1)
         match = jnp.concatenate(
             [matches(jnp.where(high == block * per + part, low, -1.0)) for part in range(per)],
             axis=0,
@@ -175,29 +186,152 @@
     lax.fori_loop(0, total.shape[0] // (per * 128), cell_block, 0)
 
 
-def finish_grid(state, obs_gain, norm_gain, total, count, grid, normed):
+def finish_block(block, state, obs_gain, norm_gain, total, count, grid, normed):
     lane = lax.broadcasted_iota(I32, count.shape, 1)
-
-    def block_of(block, _):
-        at = pl.ds(pl.multiple_of(block * 128, 128), 128)
-        number = jnp.sum(jnp.where(lane == block, count[...], 0.0), axis=1, keepdims=True)
-        number = jnp.maximum(number, 1.0)
-        value = state[at, :].astype(F32) + obs_gain[...] * (total[at, :] * (1.0 / number))
-        rounded = value.astype(BF16)
-        grid[at, :] = rounded
-        value = rounded.astype(F32)
-        scale = lax.rsqrt(jnp.mean(value * value, axis=1, keepdims=True) + EPS)
-        normed[at, :] = (value * scale * norm_gain[...]).astype(BF16)
-        return 0
-
-    lax.fori_loop(0, total.shape[0] // 128, block_of, 0)
+    at = pl.ds(pl.multiple_of(block * 128, 128), 128)
+    number = jnp.sum(jnp.where(lane == block, count[...], 0.0), axis=1, keepdims=True)
+    number = jnp.maximum(number, 1.0)
+    value = state[at, :].astype(F32) + obs_gain[...] * (total[at, :] * (1.0 / number))
+    rounded = value.astype(BF16)
+    grid[at, :] = rounded
+    value = rounded.astype(F32)
+    scale = lax.rsqrt(jnp.mean(value * value, axis=1, keepdims=True) + EPS)
+    normed[at, :] = (value * scale * norm_gain[...]).astype(BF16)
+
+
+class Halo:
+    def __init__(
+        self, barrier, normed, north, south, seam, edges, east_block, seam_out, above, below,
+        from_east, seam_in, up_sems, down_sems, east_send, east_recv, seam_send, seam_recv,
+    ):
+        faces, tiles = lax.axis_size("face"), lax.axis_size("tile")
+        face, tile = lax.axis_index("face"), lax.axis_index("tile")
+        cell_count, width = normed.shape
+        side = above.shape[0]
+        rows = cell_count // side
+        following, preceding = lax.rem(face + 1, faces), lax.rem(face + faces - 1, faces)
+        is_first, is_last = tile == 0, tile == tiles - 1
+
+        def remote(source, target, send_sem, recv_sem, device):
+            return pltpu.make_async_remote_copy(
+                src_ref=source, dst_ref=target, send_sem=send_sem, recv_sem=recv_sem,
+                device_id=device, device_id_type=MESH,
+            )
+
+        up = remote(
+            edges.at[0], below, up_sems.at[0], up_sems.at[1], (face, jnp.maximum(tile - 1, 0))
+        )
+        down = remote(
+            edges.at[1], above, down_sems.at[0], down_sems.at[1],
+            (face, jnp.minimum(tile + 1, tiles - 1)),
+        )
+
+        def east(other, device):
+            return remote(
+                east_block, from_east.at[tiles - 1 - other], east_send, east_recv.at[other], device
+            )
+
+        def seam_copy(other, device):
+            return remote(
+                seam_out.at[other], seam_in, seam_send.at[other], seam_recv, device
+            )
+
+        def each_tile(body):
+            def one(other, _):
+                body(other)
+                return 0
+
+            lax.fori_loop(0, tiles, one, 0)
+
+        def greet_one(who):
+            pl.semaphore_signal(barrier, inc=1, device_id=who, device_id_type=MESH)
+
+        def greet():
+            greet_one((following, 0))
+
+            @pl.when(jnp.logical_not(is_first))
+            def _():
+                greet_one((face, tile - 1))
+
+            @pl.when(jnp.logical_not(is_last))
+            def _():
+                greet_one((face, tile + 1))
+
+            @pl.when(is_first)
+            def _():
+                each_tile(lambda other: greet_one((preceding, other)))
+
+            return 1 + jnp.where(is_first, tiles, 1) + jnp.where(is_last, 0, 1)
+
+        def start_first():
+            edges[0] = normed[0:side, :]
+
+            @pl.when(is_first)
+            def _():
+                slot = lax.broadcasted_iota(I32, (tiles * UNIT, side), 0)
+                want = side - 1 - (slot // UNIT * rows - 1 + slot % UNIT)
+                chosen = ones_where(lax.broadcasted_iota(I32, (tiles * UNIT, side), 1) == want)
+                seam_out[...] = dot(chosen.astype(BF16), edges[0]).astype(BF16).reshape(
+                    tiles, UNIT, width
+                )
+                each_tile(lambda other: seam_copy(other, (preceding, other)).start())
+
+            @pl.when(jnp.logical_not(is_first))
+            def _():
+                up.start()
+
+        def start_last():
+            edges[1] = normed[cell_count - side : cell_count, :]
+
+            @pl.when(jnp.logical_not(is_last))
+            def _():
+                down.start()
+
+            for row in range(rows):
+                last = normed[(rows - row) * side - 16 : (rows - row) * side, :].astype(F32)
+                east_block[row : row + 1, :] = last[15:16, :]
+            east(tile, (following, 0)).start()
+
+        def finish():
+            @pl.when(jnp.logical_not(is_last))
+            def _():
+                up.wait_recv()
+                south[...] = below[...]
+                down.wait_send()
+
+            @pl.when(is_last)
+            def _():
+                south[...] = jnp.zeros_like(south)
+
+            @pl.when(jnp.logical_not(is_first))
+            def _():
+                down.wait_recv()
+                north[...] = above[...]
+                up.wait_send()
+
+            east(tile, (following, 0)).wait_send()
+            seam_copy(0, (following, 0)).wait_recv()
+            seam[...] = seam_in[...].astype(F32)
+
+            @pl.when(is_first)
+            def _():
+                def one(other):
+                    seam_copy(other, (preceding, other)).wait_send()
+                    east(other, (preceding, other)).wait_recv()
+
+                each_tile(one)
+                north[...] = from_east[...].reshape(side, width).astype(BF16)
+
+        self.greet, self.finish = greet, finish
+        self.start_first, self.start_last = start_first, start_last
 
 
 def gather_kernel(
-    send, cells, state, weight, bias, obs_gain, norm_gain, grid, normed,
-    held, cell_held, cell_flat, spots, embed, total, count,
-    send_sems, recv_sems, own_sems,
+    send, cells, state, weight, bias, obs_gain, norm_gain, grid, normed, north, south, seam,
+    held, cell_held, cell_flat, spots, embed_even, embed_odd, total, count,
+    send_sems, recv_sems, own_sems, *halo_scratch,
 ):
+    embeds = (embed_even, embed_odd)
     parts = send.shape[0]
     face, tile = lax.axis_index("face"), lax.axis_index("tile")
     sizes = send.shape[1:4]
@@ -217,6 +351,9 @@
             return 0
 
         lax.fori_loop(1, sizes[dim], greet, 0)
+
+    halo = Halo(barrier, normed, north, south, seam, *halo_scratch)
+    partners = halo.greet()
 
     def dim_of(part, stage):
         return (part + stage) % 3
@@ -273,25 +410,31 @@
             finish(part, stage)
             start(part, stage + 1)
 
-    def add(part, _=None):
-        feats = held[2, part].reshape(-1, send.shape[-1])
-        add_part(feats, spots.at[part], weight, bias, embed, total, count)
+    def embed_part(part, block):
+        feats = held.at[2, part]
+        flat = feats.reshape(sizes[0] * sizes[1] * sizes[2], UNIT, send.shape[-1])
+        embed_block(flat, block, weight, bias, embeds[part % 2])
+
+    def add(part, _=None, more=True):
+        def beside(block):
+            if more:
+                embed_part(part + 1, block)
+
+        add_part(spots.at[part], embeds[part % 2], total, count, beside)
         return 0
 
     early, late = list(range(parts // 2)), list(range(parts // 2, parts))
-    pl.semaphore_wait(barrier, sum(sizes) - 3)
+    pl.semaphore_wait(barrier, sum(sizes) - 3 + partners)
     start(parts, 0)
     for part in early:
-        start(part, 0)
-    for part in late:
         start(part, 0)
     total[...] = jnp.zeros_like(total)
     count[...] = jnp.zeros_like(count)
     advance([parts], 0)
     advance(early, 0)
     advance([parts], 1)
-    advance(early, 1)
-    advance(late, 0)
+    for part in late:
+        start(part, 0)
     finish(parts, 2)
 
     def lay(row, _):
@@ -302,195 +445,72 @@
         return 0
 
     lax.fori_loop(0, cell_flat.shape[0], lay, 0)
+    advance(early, 1)
     for part in range(parts):
         spots[part] = spread_cells(cell_flat[...], part)
-    finish(early[0], 2)
-    add(early[0])
+    for part in early:
+        finish(part, 2)
+    advance(late, 0)
+    for block in range(4):
+        embed_part(0, block)
+    add(0)
     advance(late, 1)
-    for part in early[1:]:
-        finish(part, 2)
-    lax.fori_loop(early[1], early[-1] + 1, add, 0)
+    for part in early[1:-1]:
+        add(part)
     for part in late:
         finish(part, 2)
-    lax.fori_loop(late[0], late[-1] + 1, add, 0)
-    finish_grid(state, obs_gain, norm_gain, total, count, grid, normed)
-
-
-def assimilate(send, cells, state, weight, bias, obs_gain, norm_gain):
+    for part in [early[-1]] + late[:-1]:
+        add(part)
+    add(late[-1], more=False)
+
+    def finish_grid(block):
+        finish_block(block, state, obs_gain, norm_gain, total, count, grid, normed)
+
+    def last_half(row, _):
+        finish_grid(2 * row + 1)
+        return 0
+
+    def first_half(row, _):
+        finish_grid(2 * row)
+        return 0
+
+    rows = total.shape[0] // 256
+    last_half(0, 0)
+    first_half(0, 0)
+    halo.start_first()
+    lax.fori_loop(1, rows, last_half, 0, unroll=rows - 1)
+    first_half(rows - 1, 0)
+    halo.start_last()
+    lax.fori_loop(1, rows - 1, first_half, 0, unroll=rows - 2)
+    halo.finish()
+
+
+def assimilate(send, cells, state, weight, bias, obs_gain, norm_gain, tiles, rows):
     cell_count, width = state.shape
+    side = cell_count // rows
     parts = send.shape[0]
     sources = cells.shape[0] * cells.shape[1] * cells.shape[2]
     vmem = pl.BlockSpec(memory_space=pltpu.VMEM)
     longest = max(send.shape[1:4])
     return pl.pallas_call(
         gather_kernel,
-        out_shape=(jax.ShapeDtypeStruct(state.shape, BF16),) * 2,
+        out_shape=(jax.ShapeDtypeStruct(state.shape, BF16),) * 2
+        + (jax.ShapeDtypeStruct((side, width), BF16),) * 2
+        + (jax.ShapeDtypeStruct((UNIT, width), F32),),
         in_specs=[vmem] * 7,
-        out_specs=[vmem] * 2,
+        out_specs=[vmem] * 5,
         scratch_shapes=[
             pltpu.VMEM((3,) + send.shape, BF16),
             pltpu.VMEM((3,) + cells.shape, I32),
             pltpu.VMEM((sources, 128), I32),
             pltpu.VMEM((parts, sources // 8, 128), I32),
             pltpu.VMEM((sources * UNIT, width), BF16),
+            pltpu.VMEM((sources * UNIT, width), BF16),
             pltpu.VMEM((cell_count, width), F32),
             pltpu.VMEM((128, 128), F32),
             pltpu.SemaphoreType.DMA((parts * 3 + 3, longest)),
             pltpu.SemaphoreType.DMA((parts * 3 + 3, longest)),
             pltpu.SemaphoreType.DMA((parts * 3 + 3,)),
-        ],
-        compiler_params=pltpu.CompilerParams(
-            collective_id=0, has_side_effects=True, vmem_limit_bytes=34 * MIB
-        ),
-        name="gather",
-    )(send, cells, state, weight, bias, obs_gain, norm_gain)
-
-
-def halo_kernel(
-    normed, north, south, seam, edges, east_block, seam_out, above, below, from_east, seam_in,
-    up_sems, down_sems, east_send, east_recv, seam_send, seam_recv,
-):
-    faces, tiles = lax.axis_size("face"), lax.axis_size("tile")
-    face, tile = lax.axis_index("face"), lax.axis_index("tile")
-    cell_count, width = normed.shape
-    side = above.shape[0]
-    rows = cell_count // side
-    following, preceding = lax.rem(face + 1, faces), lax.rem(face + faces - 1, faces)
-    is_first, is_last = tile == 0, tile == tiles - 1
-    barrier = pltpu.get_barrier_semaphore()
-
-    def greet(who):
-        pl.semaphore_signal(barrier, inc=1, device_id=who, device_id_type=MESH)
-
-    greet((following, 0))
-
-    @pl.when(jnp.logical_not(is_first))
-    def _():
-        greet((face, tile - 1))
-
-    @pl.when(jnp.logical_not(is_last))
-    def _():
-        greet((face, tile + 1))
-
-    @pl.when(is_first)
-    def _():
-        def one(other, _):
-            greet((preceding, other))
-            return 0
-
-        lax.fori_loop(0, tiles, one, 0)
-
-    edges[0] = normed[0:side, :]
-    edges[1] = normed[cell_count - side : cell_count, :]
-    for row in range(rows):
-        last = normed[(rows - row) * side - 16 : (rows - row) * side, :].astype(F32)
-        east_block[row : row + 1, :] = last[15:16, :]
-
-    @pl.when(is_first)
-    def _():
-        slot = lax.broadcasted_iota(I32, (tiles * UNIT, side), 0)
-        want = side - 1 - (slot // UNIT * rows - 1 + slot % UNIT)
-        chosen = ones_where(lax.broadcasted_iota(I32, (tiles * UNIT, side), 1) == want)
-        seam_out[...] = dot(chosen.astype(BF16), normed[0:side, :]).astype(BF16).reshape(
-            tiles, UNIT, width
-        )
-
-    partners = 1 + jnp.where(is_first, tiles, 1) + jnp.where(is_last, 0, 1)
-    pl.semaphore_wait(barrier, partners)
-
-    up = pltpu.make_async_remote_copy(
-        src_ref=edges.at[0], dst_ref=below,
-        send_sem=up_sems.at[0], recv_sem=up_sems.at[1],
-        device_id=(face, jnp.maximum(tile - 1, 0)), device_id_type=MESH,
-    )
-    down = pltpu.make_async_remote_copy(
-        src_ref=edges.at[1], dst_ref=above,
-        send_sem=down_sems.at[0], recv_sem=down_sems.at[1],
-        device_id=(face, jnp.minimum(tile + 1, tiles - 1)), device_id_type=MESH,
-    )
-    east = pltpu.make_async_remote_copy(
-        src_ref=east_block, dst_ref=from_east.at[tiles - 1 - tile],
-        send_sem=east_send, recv_sem=east_recv.at[tile],
-        device_id=(following, 0), device_id_type=MESH,
-    )
-
-    def seam_copy(other):
-        return pltpu.make_async_remote_copy(
-            src_ref=seam_out.at[other], dst_ref=seam_in,
-            send_sem=seam_send.at[other], recv_sem=seam_recv,
-            device_id=(preceding, other), device_id_type=MESH,
-        )
-
-    @pl.when(is_first)
-    def _():
-        def one(other, _):
-            seam_copy(other).start()
-            return 0
-
-        lax.fori_loop(0, tiles, one, 0)
-
-    east.start()
-
-    @pl.when(jnp.logical_not(is_first))
-    def _():
-        up.start()
-
-    @pl.when(jnp.logical_not(is_last))
-    def _():
-        down.start()
-
-    @pl.when(jnp.logical_not(is_last))
-    def _():
-        up.wait_recv()
-        south[...] = below[...]
-        down.wait_send()
-
-    @pl.when(is_last)
-    def _():
-        south[...] = jnp.zeros_like(south)
-
-    @pl.when(jnp.logical_not(is_first))
-    def _():
-        down.wait_recv()
-        north[...] = above[...]
-        up.wait_send()
-
-    east.wait_send()
-    pltpu.make_async_remote_copy(
-        src_ref=seam_out.at[0], dst_ref=seam_in,
-        send_sem=seam_send.at[0], recv_sem=seam_recv,
-        device_id=(following, 0), device_id_type=MESH,
-    ).wait_recv()
-    seam[...] = seam_in[...].astype(F32)
-
-    @pl.when(is_first)
-    def _():
-        def one(other, _):
-            seam_copy(other).wait_send()
-            pltpu.make_async_remote_copy(
-                src_ref=east_block, dst_ref=from_east.at[tiles - 1 - other],
-                send_sem=east_send, recv_sem=east_recv.at[other],
-                device_id=(preceding, other), device_id_type=MESH,
-            ).wait_recv()
-            return 0
-
-        lax.fori_loop(0, tiles, one, 0)
-        north[...] = from_east[...].reshape(side, width).astype(BF16)
-
-
-def exchange_halo(normed, tiles, rows):
-    cell_count, width = normed.shape
-    side = cell_count // rows
-    return pl.pallas_call(
-        halo_kernel,
-        out_shape=(
-            jax.ShapeDtypeStruct((side, width), BF16),
-            jax.ShapeDtypeStruct((side, width), BF16),
-            jax.ShapeDtypeStruct((UNIT, width), F32),
-        ),
-        in_specs=[pl.BlockSpec(memory_space=pltpu.VMEM)],
-        out_specs=[pl.BlockSpec(memory_space=pltpu.VMEM)] * 3,
-        scratch_shapes=[
             pltpu.VMEM((2, side, width), BF16),
             pltpu.VMEM((rows, width), F32),
             pltpu.VMEM((tiles, UNIT, width), BF16),
@@ -506,10 +526,10 @@
             pltpu.SemaphoreType.DMA,
         ],
         compiler_params=pltpu.CompilerParams(
-            collective_id=1, has_side_effects=True, vmem_limit_bytes=16 * MIB
+            collective_id=0, has_side_effects=True, vmem_limit_bytes=38 * MIB
         ),
-        name="halo",
-    )(normed)
+        name="gather",
+    )(send, cells, state, weight, bias, obs_gain, norm_gain)
 
 
 def encode_kernel(
@@ -518,7 +538,7 @@
     side, width = north.shape
     cells = normed.shape[0]
     rows = cells // side
-    per = 2
+    per = 4
     hidden_step = 512
 
     def put(row, values):
@@ -553,7 +573,7 @@
         result = mid
         for part in range(mlp_in.shape[1] // hidden_step):
             at = slice(part * hidden_step, (part + 1) * hidden_step)
-            hidden = gelu(dot(normed_two, mlp_in[:, at])).astype(BF16)
+            hidden = gelu_narrow(dot(normed_two, mlp_in[:, at]))
             result = result + dot(hidden, mlp_out[at, :])
         out[pl.ds(first, per * side), :] = result.astype(BF16)
         return 0
@@ -600,7 +620,7 @@
     )
     faces = lax.axis_size("face")
     across = (faces, 4, tiles // 4)
-    grid, normed = assimilate(
+    grid, normed, north, south, seam = assimilate(
         send.reshape(send.shape[:1] + across + send.shape[2:]),
         cells.reshape(across + (1, 128)),
         state.reshape(rows * side, width),
@@ -608,8 +628,9 @@
         obs_bias.reshape(1, width),
         obs_gain.reshape(1, width),
         norm_gain.reshape(1, width),
+        tiles,
+        rows,
     )
-    north, south, seam = exchange_halo(normed, tiles, rows)
     result = encode(
         normed,
         north,

time: 134 us -> 126 us (0.940)
  Pallas kernels: 128 us -> 120 us
    pallas_call x1 -> x0, Pallas kernels: 12 us -> none  [exchange_halo(): pl.pallas_call(halo_kernel, out_shape=(jax.ShapeDtypeStruct((side, width)...]
    pallas_call x1, Pallas kernels: 82.5 us -> 89.1 us  [assimilate(): pl.pallas_call(gather_kernel, out_shape=(jax.ShapeDtypeStruct(state.shape...]
    pallas_call x1, Pallas kernels: 24.6 us -> 21.8 us  [encode(): pl.pallas_call(encode_kernel, out_shape=jax.ShapeDtypeStruct(normed.shape...]
    unnamed x26 -> x24, local copies, waits for them, and re-layouts: 5.66 us -> 5.1 us
where the time goes in v4:
time: 126 us; the launch traced here: 125 us
  Pallas kernels  120 us (95%)
  local copies, waits for them, and re-layouts  5.1 us (4%)
    pallas_call x1, Pallas kernels, assimilate(): pl.pallas_call(gather_kernel, out_shape=(jax.ShapeDtypeStruct(state.shape...  89.1 us
    pallas_call x1, Pallas kernels, encode(): pl.pallas_call(encode_kernel, out_shape=jax.ShapeDtypeStruct(normed.shape...  21.8 us
    pallas_call x1, Pallas kernels, pack(): pl.pallas_call(cut_kernel, out_shape=jax.ShapeDtypeStruct((capacity // UN...  7.78 us
    unnamed x24, local copies, waits for them, and re-layouts  5.1 us

profile of v4, /device:TPU:0, one launch (start us, length us, event | category | flops | bytes accessed | tf_op | source)
XLA Modules:
  0.0 125.3 jit_solution(13974492579053645519)
XLA Ops:
  0.0 0.0 copy-start.10
  0.0 0.0 copy-start.9
  0.0 0.0 copy-start.8
  0.0 0.0 copy-start.6
  0.0 0.7 copy-done.6
  0.8 0.0 copy-start.7
  0.8 0.7 copy-done.7
  1.5 1.4 %rank.1 = (s32[1,3072]{1,0:T(1,128)S(1)}, s32[1,128]{1,0:T(1,128)S(1)}, s32[128,128]{1,0:T(8,128)S(1)}) custom-call(s32[1,3072]{1,0:T(1,128)S(1)} %bitcast.15, s32[1,3072]{1,0:T(1,128)S(1)} %bitcast.16), custom_call_target="tpu_custom_call" | custom-call | tf_op jit(solution)/shard_map/rank/pallas_call | solution.py:108
  2.9 0.0 copy-start.4
  2.9 1.1 copy-done.4
  4.0 0.0 copy-start.1
  4.0 0.0 copy-start.2
  4.0 7.8 %cut.1 = bf16[6,128,16,128]{3,2,1,0:T(8,128)(2,1)S(1)} custom-call(s32[1,128]{1,0:T(1,128)S(1)} %get-tuple-element.13.starts, s32[1,3072]{1,0:T(1,128)S(1)} %get-tuple-element.14.rank, bf16[3072,128]{1,0:T(8,128)(2,1)S(1)} %copy-done.4), custom_call_target="tpu_custom_call" | custom-call | tf_op jit(solution)/shard_map/cut/pallas_call | solution.py:120
  11.8 0.0 copy-done.10
  11.8 0.0 copy-done.9
  11.8 0.0 copy-done.8
  11.8 0.0 copy-start.3
  11.8 1.6 %copy-done.3 = bf16[1,1,8,256,512]{4,3,2,1,0:T(8,128)(2,1)S(1)} copy-done((bf16[1,1,8,256,512]{4,3,2,1,0:T(8,128)(2,1)S(1)}, bf16[1,1,8,256,512]{4,3,2,1,0:T(8,128)(2,1)}, u32[]{:S(2)}) %copy-start.3) | copy-done | bytes 2097176
  13.4 0.0 copy-start.5
  13.4 0.9 copy-done.5
  14.3 0.0 copy-start
  14.3 0.0 copy-start.11
  14.3 89.1 %gather.1 = (bf16[2048,512]{1,0:T(8,128)(2,1)S(1)}, bf16[2048,512]{1,0:T(8,128)(2,1)S(1)}, bf16[256,512]{1,0:T(8,128)(2,1)S(1)}, bf16[256,512]{1,0:T(8,128)(2,1)S(1)}, f32[16,512]{1,0:T(8,128)S(1)}) custom-call(bf16[6,4,4,8,16,128]{5,4,3,2,1,0:T(8,128)(2,1)S(1)} %bitcast.11, s32[4,4,8,1,128]{4,3,2,1,0:T(1,128)S(1)} %bitcast.14, ...), custom_call_target="tpu_custom_call" | custom-call | tf_op jit(solution)/shard_map/gather/pallas_call | solution.py:495
  103.5 0.0 copy-done.1
  103.5 0.0 copy-done.2
  103.5 0.0 copy-done
  103.5 0.0 copy-done.11
  103.5 21.8 %encode.1 = bf16[2048,512]{1,0:T(8,128)(2,1)} custom-call(bf16[2048,512]{1,0:T(8,128)(2,1)S(1)} %get-tuple-element.16.normed, bf16[256,512]{1,0:T(8,128)(2,1)S(1)} %get-tuple-element.17.north, bf16[256,512]{1,0:T(8,128)(2,1)S(1)} %get-tuple-element.18.south, f32[16,512]{1,0:T(8,128)S(1)} %get-tuple-element.19.seam, ...), custom_call_target="tpu_custom_call" | custom-call | tf_op jit(solution)/shard_map/encode/pallas_call | solution.py:588
Async XLA Ops:
  0.0 11.8 %copy-start.10 = (f32[512]{0:T(512)S(1)}, f32[512]{0:T(512)}, u32[]{:S(2)}) copy-start(f32[512]{0:T(512)} %param.19) | copy-start | bytes 6148
  0.0 11.8 %copy-start.9 = (f32[512]{0:T(512)S(1)}, f32[512]{0:T(512)}, u32[]{:S(2)}) copy-start(f32[512]{0:T(512)} %param.18) | copy-start | bytes 6148
  0.0 11.8 %copy-start.8 = (f32[512]{0:T(512)S(1)}, f32[512]{0:T(512)}, u32[]{:S(2)}) copy-start(f32[512]{0:T(512)} %param.17) | copy-start | bytes 6148
  0.0 0.7 copy-start.6
  0.8 0.7 copy-start.7
  2.9 1.1 copy-start.4
  4.0 99.5 %copy-start.1 = (bf16[512,2048]{1,0:T(8,128)(2,1)S(1)}, bf16[512,2048]{1,0:T(8,128)(2,1)}, u32[]{:S(2)}) copy-start(bf16[512,2048]{1,0:T(8,128)(2,1)} %mlp_in.1) | copy-start | bytes 6291460
  4.0 99.5 %copy-start.2 = (bf16[2048,512]{1,0:T(8,128)(2,1)S(1)}, bf16[2048,512]{1,0:T(8,128)(2,1)}, u32[]{:S(2)}) copy-start(bf16[2048,512]{1,0:T(8,128)(2,1)} %mlp_out.1) | copy-start | bytes 6291460
  11.8 1.6 %copy-start.3 = (bf16[1,1,8,256,512]{4,3,2,1,0:T(8,128)(2,1)S(1)}, bf16[1,1,8,256,512]{4,3,2,1,0:T(8,128)(2,1)}, u32[]{:S(2)}) copy-start(bf16[1,1,8,256,512]{4,3,2,1,0:T(8,128)(2,1)} %param.12) | copy-start | bytes 6291460
  13.4 0.9 copy-start.5
  14.3 89.2 %copy-start = (bf16[9,512,512]{2,1,0:T(8,128)(2,1)S(1)}, bf16[9,512,512]{2,1,0:T(8,128)(2,1)}, u32[]{:S(2)}) copy-start(bf16[9,512,512]{2,1,0:T(8,128)(2,1)} %param.20) | copy-start | bytes 14155780
  14.3 89.2 %copy-start.11 = (f32[512]{0:T(512)S(1)}, f32[512]{0:T(512)}, u32[]{:S(2)}) copy-start(f32[512]{0:T(512)} %param.21) | copy-start | bytes 6148

commit v5 on v4

--- a/solution.py
+++ b/solution.py
@@ -81,15 +81,24 @@
     rows = feat.shape[0]
     capacity = parts * UNIT
 
+    tall = 1024
+    ids = lax.broadcasted_iota(I32, (128, 128), 0).astype(F32).astype(BF16)
+
     def sort_block(block, _):
-        first = pl.multiple_of(block * BLOCK, BLOCK)
-        chosen = ones_where(
-            lax.broadcasted_iota(I32, (BLOCK, rows), 0) + first == rank[...]
-        ).astype(BF16)
-        ordered[pl.ds(first, BLOCK), :] = dot(chosen, feat[...])
-        return 0
-
-    lax.fori_loop(0, rows // BLOCK, sort_block, 0)
+        first = pl.multiple_of(block * tall, tall)
+        chosen = []
+        for part in range(tall // 128):
+            place = rank[...] - (first + part * 128)
+            place = jnp.where((place >= 0) & (place < 128), place, -1).astype(F32)
+            chosen.append(
+                jnp.concatenate(
+                    [match_rows(ids, place[:, at : at + 128]) for at in range(0, rows, 128)], axis=1
+                )
+            )
+        ordered[pl.ds(first, tall), :] = dot(jnp.concatenate(chosen, axis=0), feat[...])
+        return 0
+
+    lax.fori_loop(0, rows // tall, sort_block, 0)
     ordered[rows:, :] = jnp.zeros((ordered.shape[0] - rows, feat.shape[1]), F32)
 
     def cut(target, _):
@@ -123,7 +132,7 @@
         in_specs=[pl.BlockSpec(memory_space=pltpu.SMEM), vmem, vmem],
         out_specs=vmem,
         scratch_shapes=[pltpu.VMEM((rows + 2 * capacity, width), F32)],
-        compiler_params=pltpu.CompilerParams(vmem_limit_bytes=16 * MIB),
+        compiler_params=pltpu.CompilerParams(vmem_limit_bytes=24 * MIB),
         name="cut",
     )(starts, rank, feat)
     return send, cells
@@ -539,7 +548,7 @@
     cells = normed.shape[0]
     rows = cells // side
     per = 4
-    hidden_step = 512
+    hidden_step = 1024
 
     def put(row, values):
         values = values.astype(F32)

time: 126 us -> 124 us (0.984)
    pallas_call x1, Pallas kernels: 7.78 us -> 6.38 us  [pack(): pl.pallas_call(cut_kernel, out_shape=jax.ShapeDtypeStruct((capacity // UN...]
where the time goes in v5:
time: 124 us
  Pallas kernels  119 us (96%)
  local copies, waits for them, and re-layouts  5.1 us (4%)
    pallas_call x1, Pallas kernels, assimilate(): pl.pallas_call(gather_kernel, out_shape=(jax.ShapeDtypeStruct(state.shape...  89.2 us
    pallas_call x1, Pallas kernels, encode(): pl.pallas_call(encode_kernel, out_shape=jax.ShapeDtypeStruct(normed.shape...  21.7 us
    pallas_call x1, Pallas kernels, pack(): pl.pallas_call(cut_kernel, out_shape=jax.ShapeDtypeStruct((capacity // UN...  6.38 us
    unnamed x24, local copies, waits for them, and re-layouts  5.1 us

profile of v5, /device:TPU:0, one launch (start us, length us, event | category | flops | bytes accessed | tf_op | source)
XLA Modules:
  0.0 123.8 jit_solution(1275701451307969176)
XLA Ops:
  0.0 0.0 copy-start.10
  0.0 0.0 copy-start.9
  0.0 0.0 copy-start.8
  0.0 0.0 copy-start.6
  0.0 0.7 copy-done.6
  0.8 0.0 copy-start.7
  0.8 0.7 copy-done.7
  1.5 1.4 %rank.1 = (s32[1,3072]{1,0:T(1,128)S(1)}, s32[1,128]{1,0:T(1,128)S(1)}, s32[128,128]{1,0:T(8,128)S(1)}) custom-call(s32[1,3072]{1,0:T(1,128)S(1)} %bitcast.15, s32[1,3072]{1,0:T(1,128)S(1)} %bitcast.16), custom_call_target="tpu_custom_call" | custom-call | tf_op jit(solution)/shard_map/rank/pallas_call | solution.py:117
  2.9 0.0 copy-start.4
  2.9 1.1 copy-done.4
  4.0 0.0 copy-start.1
  4.0 0.0 copy-start.2
  4.0 6.4 %cut.1 = bf16[6,128,16,128]{3,2,1,0:T(8,128)(2,1)S(1)} custom-call(s32[1,128]{1,0:T(1,128)S(1)} %get-tuple-element.13.starts, s32[1,3072]{1,0:T(1,128)S(1)} %get-tuple-element.14.rank, bf16[3072,128]{1,0:T(8,128)(2,1)S(1)} %copy-done.4), custom_call_target="tpu_custom_call" | custom-call | tf_op jit(solution)/shard_map/cut/pallas_call | solution.py:129
  10.4 0.0 copy-done.10
  10.4 0.0 copy-done.9
  10.4 0.0 copy-done.8
  10.4 0.0 copy-start.3
  10.4 1.6 %copy-done.3 = bf16[1,1,8,256,512]{4,3,2,1,0:T(8,128)(2,1)S(1)} copy-done((bf16[1,1,8,256,512]{4,3,2,1,0:T(8,128)(2,1)S(1)}, bf16[1,1,8,256,512]{4,3,2,1,0:T(8,128)(2,1)}, u32[]{:S(2)}) %copy-start.3) | copy-done | bytes 2097176
  12.0 0.0 copy-start.5
  12.0 0.9 copy-done.5
  12.9 0.0 copy-start
  12.9 0.0 copy-start.11
  12.9 89.2 %gather.1 = (bf16[2048,512]{1,0:T(8,128)(2,1)S(1)}, bf16[2048,512]{1,0:T(8,128)(2,1)S(1)}, bf16[256,512]{1,0:T(8,128)(2,1)S(1)}, bf16[256,512]{1,0:T(8,128)(2,1)S(1)}, f32[16,512]{1,0:T(8,128)S(1)}) custom-call(bf16[6,4,4,8,16,128]{5,4,3,2,1,0:T(8,128)(2,1)S(1)} %bitcast.11, s32[4,4,8,1,128]{4,3,2,1,0:T(1,128)S(1)} %bitcast.14, ...), custom_call_target="tpu_custom_call" | custom-call | tf_op jit(solution)/shard_map/gather/pallas_call | solution.py:504
  102.1 0.0 copy-done.1
  102.1 0.0 copy-done.2
  102.1 0.0 copy-done
  102.2 0.0 copy-done.11
  102.2 21.7 %encode.1 = bf16[2048,512]{1,0:T(8,128)(2,1)} custom-call(bf16[2048,512]{1,0:T(8,128)(2,1)S(1)} %get-tuple-element.16.normed, bf16[256,512]{1,0:T(8,128)(2,1)S(1)} %get-tuple-element.17.north, bf16[256,512]{1,0:T(8,128)(2,1)S(1)} %get-tuple-element.18.south, f32[16,512]{1,0:T(8,128)S(1)} %get-tuple-element.19.seam, ...), custom_call_target="tpu_custom_call" | custom-call | tf_op jit(solution)/shard_map/encode/pallas_call | solution.py:597
Async XLA Ops:
  0.0 10.4 %copy-start.10 = (f32[512]{0:T(512)S(1)}, f32[512]{0:T(512)}, u32[]{:S(2)}) copy-start(f32[512]{0:T(512)} %param.19) | copy-start | bytes 6148
  0.0 10.4 %copy-start.9 = (f32[512]{0:T(512)S(1)}, f32[512]{0:T(512)}, u32[]{:S(2)}) copy-start(f32[512]{0:T(512)} %param.18) | copy-start | bytes 6148
  0.0 10.4 %copy-start.8 = (f32[512]{0:T(512)S(1)}, f32[512]{0:T(512)}, u32[]{:S(2)}) copy-start(f32[512]{0:T(512)} %param.17) | copy-start | bytes 6148
  0.0 0.7 copy-start.6
  0.8 0.7 copy-start.7
  2.9 1.1 copy-start.4
  4.0 98.1 %copy-start.1 = (bf16[512,2048]{1,0:T(8,128)(2,1)S(1)}, bf16[512,2048]{1,0:T(8,128)(2,1)}, u32[]{:S(2)}) copy-start(bf16[512,2048]{1,0:T(8,128)(2,1)} %mlp_in.1) | copy-start | bytes 6291460
  4.0 98.1 %copy-start.2 = (bf16[2048,512]{1,0:T(8,128)(2,1)S(1)}, bf16[2048,512]{1,0:T(8,128)(2,1)}, u32[]{:S(2)}) copy-start(bf16[2048,512]{1,0:T(8,128)(2,1)} %mlp_out.1) | copy-start | bytes 6291460
  10.4 1.6 %copy-start.3 = (bf16[1,1,8,256,512]{4,3,2,1,0:T(8,128)(2,1)S(1)}, bf16[1,1,8,256,512]{4,3,2,1,0:T(8,128)(2,1)}, u32[]{:S(2)}) copy-start(bf16[1,1,8,256,512]{4,3,2,1,0:T(8,128)(2,1)} %param.12) | copy-start | bytes 6291460
  12.0 0.9 copy-start.5
  12.9 89.2 %copy-start = (bf16[9,512,512]{2,1,0:T(8,128)(2,1)S(1)}, bf16[9,512,512]{2,1,0:T(8,128)(2,1)}, u32[]{:S(2)}) copy-start(bf16[9,512,512]{2,1,0:T(8,128)(2,1)} %param.20) | copy-start | bytes 14155780
  12.9 89.2 %copy-start.11 = (f32[512]{0:T(512)S(1)}, f32[512]{0:T(512)}, u32[]{:S(2)}) copy-start(f32[512]{0:T(512)} %param.21) | copy-start | bytes 6148

commit v6 on v5

--- a/solution.py
+++ b/solution.py
@@ -444,6 +444,7 @@
     advance([parts], 1)
     for part in late:
         start(part, 0)
+    advance(early, 1)
     finish(parts, 2)
 
     def lay(row, _):
@@ -453,8 +454,7 @@
         ]
         return 0
 
-    lax.fori_loop(0, cell_flat.shape[0], lay, 0)
-    advance(early, 1)
+    lax.fori_loop(0, cell_flat.shape[0], lay, 0, unroll=4)
     for part in range(parts):
         spots[part] = spread_cells(cell_flat[...], part)
     for part in early:

time: 124 us -> 123 us (level)
  Pallas kernels: 119 us -> 117 us
    pallas_call x1, Pallas kernels: 89.2 us -> 87.8 us  [assimilate(): pl.pallas_call(gather_kernel, out_shape=(jax.ShapeDtypeStruct(state.shape...]
where the time goes in v6:
time: 123 us; the launch traced here: 122 us
  Pallas kernels  117 us (95%)
  local copies, waits for them, and re-layouts  5.1 us (4%)
    pallas_call x1, Pallas kernels, assimilate(): pl.pallas_call(gather_kernel, out_shape=(jax.ShapeDtypeStruct(state.shape...  87.8 us
    pallas_call x1, Pallas kernels, encode(): pl.pallas_call(encode_kernel, out_shape=jax.ShapeDtypeStruct(normed.shape...  21.7 us
    pallas_call x1, Pallas kernels, pack(): pl.pallas_call(cut_kernel, out_shape=jax.ShapeDtypeStruct((capacity // UN...  6.38 us
    unnamed x24, local copies, waits for them, and re-layouts  5.1 us

profile of v6, /device:TPU:0, one launch (start us, length us, event | category | flops | bytes accessed | tf_op | source)
XLA Modules:
  0.0 122.5 jit_solution(5891560860436192345)
XLA Ops:
  0.0 0.0 copy-start.10
  0.0 0.0 copy-start.9
  0.0 0.0 copy-start.8
  0.0 0.0 copy-start.6
  0.0 0.7 copy-done.6
  0.8 0.0 copy-start.7
  0.8 0.7 copy-done.7
  1.5 1.4 %rank.1 = (s32[1,3072]{1,0:T(1,128)S(1)}, s32[1,128]{1,0:T(1,128)S(1)}, s32[128,128]{1,0:T(8,128)S(1)}) custom-call(s32[1,3072]{1,0:T(1,128)S(1)} %bitcast.15, s32[1,3072]{1,0:T(1,128)S(1)} %bitcast.16), custom_call_target="tpu_custom_call" | custom-call | tf_op jit(solution)/shard_map/rank/pallas_call | solution.py:117
  2.9 0.0 copy-start.4
  2.9 1.1 copy-done.4
  4.0 0.0 copy-start.1
  4.0 0.0 copy-start.2
  4.0 6.4 %cut.1 = bf16[6,128,16,128]{3,2,1,0:T(8,128)(2,1)S(1)} custom-call(s32[1,128]{1,0:T(1,128)S(1)} %get-tuple-element.13.starts, s32[1,3072]{1,0:T(1,128)S(1)} %get-tuple-element.14.rank, bf16[3072,128]{1,0:T(8,128)(2,1)S(1)} %copy-done.4), custom_call_target="tpu_custom_call" | custom-call | tf_op jit(solution)/shard_map/cut/pallas_call | solution.py:129
  10.4 0.0 copy-done.10
  10.4 0.0 copy-done.9
  10.4 0.0 copy-done.8
  10.4 0.0 copy-start.3
  10.4 1.6 %copy-done.3 = bf16[1,1,8,256,512]{4,3,2,1,0:T(8,128)(2,1)S(1)} copy-done((bf16[1,1,8,256,512]{4,3,2,1,0:T(8,128)(2,1)S(1)}, bf16[1,1,8,256,512]{4,3,2,1,0:T(8,128)(2,1)}, u32[]{:S(2)}) %copy-start.3) | copy-done | bytes 2097176
  12.0 0.0 copy-start.5
  12.0 0.9 copy-done.5
  12.9 0.0 copy-start
  12.9 0.0 copy-start.11
  12.9 87.8 %gather.1 = (bf16[2048,512]{1,0:T(8,128)(2,1)S(1)}, bf16[2048,512]{1,0:T(8,128)(2,1)S(1)}, bf16[256,512]{1,0:T(8,128)(2,1)S(1)}, bf16[256,512]{1,0:T(8,128)(2,1)S(1)}, f32[16,512]{1,0:T(8,128)S(1)}) custom-call(bf16[6,4,4,8,16,128]{5,4,3,2,1,0:T(8,128)(2,1)S(1)} %bitcast.11, s32[4,4,8,1,128]{4,3,2,1,0:T(1,128)S(1)} %bitcast.14, ...), custom_call_target="tpu_custom_call" | custom-call | tf_op jit(solution)/shard_map/gather/pallas_call | solution.py:504
  100.8 0.0 copy-done.1
  100.8 0.0 copy-done.2
  100.8 0.0 copy-done
  100.8 0.0 copy-done.11
  100.8 21.7 %encode.1 = bf16[2048,512]{1,0:T(8,128)(2,1)} custom-call(bf16[2048,512]{1,0:T(8,128)(2,1)S(1)} %get-tuple-element.16.normed, bf16[256,512]{1,0:T(8,128)(2,1)S(1)} %get-tuple-element.17.north, bf16[256,512]{1,0:T(8,128)(2,1)S(1)} %get-tuple-element.18.south, f32[16,512]{1,0:T(8,128)S(1)} %get-tuple-element.19.seam, ...), custom_call_target="tpu_custom_call" | custom-call | tf_op jit(solution)/shard_map/encode/pallas_call | solution.py:597
Async XLA Ops:
  0.0 10.4 %copy-start.10 = (f32[512]{0:T(512)S(1)}, f32[512]{0:T(512)}, u32[]{:S(2)}) copy-start(f32[512]{0:T(512)} %param.19) | copy-start | bytes 6148
  0.0 10.4 %copy-start.9 = (f32[512]{0:T(512)S(1)}, f32[512]{0:T(512)}, u32[]{:S(2)}) copy-start(f32[512]{0:T(512)} %param.18) | copy-start | bytes 6148
  0.0 10.4 %copy-start.8 = (f32[512]{0:T(512)S(1)}, f32[512]{0:T(512)}, u32[]{:S(2)}) copy-start(f32[512]{0:T(512)} %param.17) | copy-start | bytes 6148
  0.0 0.7 copy-start.6
  0.8 0.7 copy-start.7
  2.9 1.1 copy-start.4
  4.0 96.8 %copy-start.1 = (bf16[512,2048]{1,0:T(8,128)(2,1)S(1)}, bf16[512,2048]{1,0:T(8,128)(2,1)}, u32[]{:S(2)}) copy-start(bf16[512,2048]{1,0:T(8,128)(2,1)} %mlp_in.1) | copy-start | bytes 6291460
  4.0 96.8 %copy-start.2 = (bf16[2048,512]{1,0:T(8,128)(2,1)S(1)}, bf16[2048,512]{1,0:T(8,128)(2,1)}, u32[]{:S(2)}) copy-start(bf16[2048,512]{1,0:T(8,128)(2,1)} %mlp_out.1) | copy-start | bytes 6291460
  10.4 1.6 %copy-start.3 = (bf16[1,1,8,256,512]{4,3,2,1,0:T(8,128)(2,1)S(1)}, bf16[1,1,8,256,512]{4,3,2,1,0:T(8,128)(2,1)}, u32[]{:S(2)}) copy-start(bf16[1,1,8,256,512]{4,3,2,1,0:T(8,128)(2,1)} %param.12) | copy-start | bytes 6291460
  12.0 0.9 copy-start.5
  12.9 87.8 %copy-start = (bf16[9,512,512]{2,1,0:T(8,128)(2,1)S(1)}, bf16[9,512,512]{2,1,0:T(8,128)(2,1)}, u32[]{:S(2)}) copy-start(bf16[9,512,512]{2,1,0:T(8,128)(2,1)} %param.20) | copy-start | bytes 14155780
  12.9 87.9 %copy-start.11 = (f32[512]{0:T(512)S(1)}, f32[512]{0:T(512)}, u32[]{:S(2)}) copy-start(f32[512]{0:T(512)} %param.21) | copy-start | bytes 6148
